TPU v7x, 32 devices: a whole 2x2x4 slice. The times are simulated.
32 devices in a mesh: sweep: 2 (over y), tm: 8 (over z, x), unit: 2 (over core).
Axes of the slice: x: 2, y: 2, z: 4, core: 2. Of those that a mesh axis runs over, the one named last changes fastest.
Arguments:
- projections: bfloat16 [2, 32, 3, 1024], P('sweep', 'tm', None, 'unit'), parts along dimension 0, may hold values from -6 to 6
- recurrent: bfloat16 [2048, 3, 1024], P('sweep', None, 'unit'), parts along dimension 0, may hold values from -0.375 to 0.375
- update_bias: float32 [2048], P(('sweep', 'unit')), parts along dimension 0, may hold values from -1 to 13
- candidate_bias: float32 [2048], P(('sweep', 'unit')), parts along dimension 0, may hold values from -5 to 5
- start_state: float32 [2, 1024], P('sweep', 'unit'), parts along dimension 0, may hold values from -4 to 4
- initial_guess: float32 [2, 32, 1024], P('sweep', 'tm', 'unit'), parts along dimension 0, may hold values from -3 to 3
Outputs:
- trajectory: float32 [2, 32, 1024], P('sweep', 'tm', 'unit'), parts along dimension 0
There are 2 independent parts, one for each index of `sweep`. A program takes and returns all parts, laid end to end along the dimension named above; each array names one. Nothing has to cross between parts.
All inputs are finite; a program needn't handle non-finite values.
Results may differ from a plain program's by a relative error of at most 0.0017.
Values may be sent and summed in bfloat16 or wider, within the bound.
A program may use at most 64 MiB of HBM per device.

v0:
```python
import jax
import jax.numpy as jnp
from jax import lax
from jax.sharding import PartitionSpec as P

BLOCK = 128
NEWTON = 2
GROUP = 8


HIGHEST_MODE = lax.Precision.HIGHEST


def passed_along(value, axis, steps):
    count = lax.axis_size(axis)
    initial, last = (max(0, -steps), min(count, count - steps))
    return lax.ppermute(value, axis, [(source, source + steps) for source in range(initial, last)])


def combine(earlier, later):
    matrix = jnp.einsum("pji,pik->pjk", later[0], earlier[0], precision=HIGHEST_MODE)
    vector = jnp.einsum("pji,pi->pj", later[0], earlier[1], precision=HIGHEST_MODE) + later[1]
    return (matrix, vector)


def apply_map(matrix, vector, current):
    return jnp.einsum("pji,pi->pj", matrix, current, precision=HIGHEST_MODE) + vector


def advance_keep(current, inputs):
    following = apply_map(inputs[0], inputs[1], current)
    return (following, following)


def advance_last(current, inputs):
    return (apply_map(inputs[0], inputs[1], current), None)


def compose(product, jac_step):
    return (jnp.einsum("pji,pik->pjk", jac_step, product, precision=HIGHEST_MODE), None)


def to_time(values, num_blocks):
    moved = jnp.transpose(values, (1, 0, 2))
    return moved.reshape(moved.shape[0], moved.shape[1], num_blocks, BLOCK)


def shards(projections, recurrent, update_bias, candidate_bias, start_state, initial_guess):
    num_batch, num_steps, _, width_dev = projections.shape
    full_width = recurrent.shape[0]
    num_blocks = width_dev // BLOCK
    num_pairs = num_batch * num_blocks
    unit_place = lax.axis_index("unit")
    time_place = lax.axis_index("tm")
    flat_weight = recurrent.reshape(full_width, 3 * width_dev)
    own_rows = lax.dynamic_slice_in_dim(recurrent, unit_place * width_dev, width_dev, 0)
    own_rows = own_rows.astype(jnp.float32).reshape(num_blocks, BLOCK, 3, num_blocks, BLOCK)
    diagonal = jnp.einsum("kigkj->gkji", own_rows)
    identity = jnp.eye(BLOCK, dtype=jnp.float32)
    start_pairs = start_state.reshape(num_pairs, BLOCK)
    last_guess = passed_along(initial_guess[:, -1, :], "tm", 1)
    entering = jnp.where(time_place == 0, start_state, last_guess)
    trajectory = initial_guess
    for newton_turn in range(NEWTON):
        previous = jnp.concatenate([entering[:, None, :], trajectory[:, :-1, :]], axis=1)
        panels = previous.astype(jnp.bfloat16).reshape(num_batch * num_steps, width_dev)
        recurrent_terms = jnp.dot(
            lax.all_gather(panels, "unit", axis=1, tiled=True),
            flat_weight,
            preferred_element_type=jnp.float32,
        )
        recurrent_terms = recurrent_terms.reshape(num_batch, num_steps, 3, width_dev)
        update_gate = jax.nn.sigmoid(
            projections[:, :, 0].astype(jnp.float32) + recurrent_terms[:, :, 0] + update_bias
        )
        reset_gate = jax.nn.sigmoid(
            projections[:, :, 1].astype(jnp.float32) + recurrent_terms[:, :, 1]
        )
        cand_rec = recurrent_terms[:, :, 2] + candidate_bias
        candidate = jnp.tanh(projections[:, :, 2].astype(jnp.float32) + reset_gate * cand_rec)
        mapped = (1.0 - update_gate) * candidate + update_gate * previous
        coef_a = to_time((previous - candidate) * update_gate * (1.0 - update_gate), num_blocks)
        coef_full = (1.0 - update_gate) * (1.0 - candidate * candidate) * reset_gate
        coef_c = to_time(coef_full * cand_rec * (1.0 - reset_gate), num_blocks)
        coef_d = to_time(coef_full, num_blocks)
        gate_time = to_time(update_gate, num_blocks)
        jacobian = (
            coef_a[..., None] * diagonal[0]
            + coef_c[..., None] * diagonal[1]
            + coef_d[..., None] * diagonal[2]
            + gate_time[..., None] * identity
        )
        jacobian = jacobian.reshape(num_steps, num_pairs, BLOCK, BLOCK)
        prev_pairs = to_time(previous, num_blocks).reshape(num_steps, num_pairs, BLOCK)
        mapped_pairs = to_time(mapped, num_blocks).reshape(num_steps, num_pairs, BLOCK)
        offsets = mapped_pairs - jnp.einsum(
            "tpji,tpi->tpj", jacobian, prev_pairs, precision=HIGHEST_MODE
        )
        stretch_matrix, _ = lax.scan(compose, jacobian[0], jacobian[1:])
        stretch_vector, _ = lax.scan(
            advance_last, jnp.zeros((num_pairs, BLOCK), jnp.float32), (jacobian, offsets)
        )
        neutral = (
            jnp.broadcast_to(identity, (num_pairs, BLOCK, BLOCK)),
            jnp.zeros((num_pairs, BLOCK), jnp.float32),
        )
        shifted = passed_along((stretch_matrix, stretch_vector), "tm", 1)
        window_matrix = jnp.where(time_place == 0, neutral[0], shifted[0])
        window_vector = jnp.where(time_place == 0, neutral[1], shifted[1])
        for level in range(GROUP.bit_length() - 1):
            window_span = 1 << level
            received = passed_along((window_matrix, window_vector), "tm", window_span)
            joined = combine(received, (window_matrix, window_vector))
            receives = time_place >= window_span
            window_matrix = jnp.where(receives, joined[0], window_matrix)
            window_vector = jnp.where(receives, joined[1], window_vector)
        entering_pairs = apply_map(window_matrix, window_vector, start_pairs)

        def relay(group_index, entering_now):
            arrived = passed_along(entering_now, "tm", GROUP)
            moved = apply_map(window_matrix, window_vector, arrived)
            return jnp.where(time_place // GROUP == group_index, moved, entering_now)

        entering_pairs = lax.fori_loop(1, lax.axis_size("tm") // GROUP, relay, entering_pairs)
        carried, states = lax.scan(advance_keep, entering_pairs, (jacobian, offsets))
        trajectory = jnp.transpose(states.reshape(num_steps, num_batch, width_dev), (1, 0, 2))
        entering = entering_pairs.reshape(num_batch, width_dev)
    return trajectory


def solution(mesh):
    return jax.shard_map(
        shards,
        mesh=mesh,
        in_specs=(
            P("sweep", "tm", None, "unit"),
            P("sweep", None, "unit"),
            P(("sweep", "unit")),
            P(("sweep", "unit")),
            P("sweep", "unit"),
            P("sweep", "tm", "unit"),
        ),
        out_specs=P("sweep", "tm", "unit"),
        check_vma=False,
    )
```

profile of v0, /device:TPU:24, one launch (start us, length us, event | category | flops | bytes accessed | tf_op | source)
XLA Modules:
  0.0 161.2 jit_solution(17687558604713067622)
XLA Ops:
  0.7 3.4 %collective-permute-start = (f32[1,512]{1,0:T(1,128)S(1)}, f32[1,512]{1,0:T(1,128)S(1)}, u32[]{:S(2)}, u32[]{:S(2)}) collective-permute-start(f32[1,512]{1,0:T(1,128)S(1)} %slice_bitcast_fusion.7), channel_id=1, source_target_pairs={{0,2},{2,4},{4,6},{6,8},{8,10},{10,12},{12,14},{1,3},{3,5},{5,7},{... | collective-permute-start | bytes 6152 | tf_op jit(solution)/shard_map/ppermute | solution.py:17
  5.5 3.5 %dynamic-slice_convert_fusion = f32[512,3,512]{2,0,1:T(8,128)} fusion(bf16[1024,3,512]{2,0,1:T(8,128)(2,1)} %param.19, s32[]{:T(128)S(6)} %select_n.104), kind=kLoop, calls=%fused_computation.37 | loop fusion | flops 786432 | bytes 4718596 | tf_op jit(solution)/shard_map/reshape | solution.py:57
  9.0 3.1 %reshape.752 = f32[4,128,3,4,128]{4,3,1,0,2:T(4,128)S(1)} reshape(f32[512,3,512]{2,0,1:T(8,128)} %dynamic-slice_convert_fusion) | data formatting | bytes 6291456 | tf_op jit(solution)/shard_map/reshape | solution.py:57
  13.0 0.9 slice_bitcast_fusion.6
  14.0 3.2 %copy.8 = bf16[1024,3,512]{0,2,1:T(8,128)(2,1)S(1)} copy(bf16[1024,3,512]{2,0,1:T(8,128)(2,1)} %param.19) | data formatting | bytes 6291456 | tf_op args[1]
  17.3 1.1 copy.9
  18.4 1.9 %copy.11 = f32[4,128,128]{2,1,0:T(8,128)} copy(f32[4,128,128]{1,0,2:T(4,128)} %get-tuple-element.240) | data formatting | bytes 524288 | tf_op jit(solution)/shard_map/mul | solution.py:90
  20.3 1.8 %copy.10 = f32[4,128,128]{2,1,0:T(8,128)} copy(f32[4,128,128]{1,0,2:T(4,128)} %get-tuple-element.241) | data formatting | bytes 524288 | tf_op jit(solution)/shard_map/mul | solution.py:89
  22.1 1.8 %all_gather.6 = bf16[4,1024]{1,0:T(4,128)(2,1)S(1)} all-gather(bf16[4,512]{1,0:T(4,128)(2,1)S(1)} %pad_maximum_fusion.2), channel_id=1, replica_groups=mesh['sweep'=2,'tm'=8,'unit'=2] {'unit'}, dimensions={1}, use_global_device_ids=true | all-gather | bytes 12288 | tf_op jit(solution)/shard_map/all_gather | solution.py:68
  24.9 2.2 %multiply_add_fusion.2 = f32[4,4,128,128]{3,2,1,0:T(8,128)S(1)} fusion(f32[128,128]{1,0:T(8,128)S(1)} %fusion.34, f32[4,4,128]{2,1,0:T(4,128)S(1)} %get-tuple-element.234, f32[4,128,128]{2,1,0:T(8,128)} %copy.11, f32[4,4,128]{2,1,0:T(4,128)S(1)} %get-tuple-element.236, f32[4,128,128]{2,1,0:T(8,128)} %copy.10, f32[4,4,128]{2,1,0:T(4,128)S(1)} %get-tuple-element.235, ...), kind=kLoop, calls=%fused_computation.48 | loop fusion | flops 1835008 | bytes 1933312 | tf_op jit(solution)/shard_map/add | solution.py:88
  27.1 2.6 %multiply_add_fusion.3 = f32[4,1,4,128,128]{4,3,2,0,1:T(8,128)S(1)} fusion(f32[128,128]{1,0:T(8,128)S(1)} %fusion.34, f32[4,4,128]{2,1,0:T(4,128)S(1)} %get-tuple-element.234, f32[4,128,128]{2,1,0:T(8,128)} %copy.11, f32[4,4,128]{2,1,0:T(4,128)S(1)} %get-tuple-element.236, f32[4,128,128]{2,1,0:T(8,128)} %copy.10, f32[4,4,128]{2,1,0:T(4,128)S(1)} %get-tuple-element.235, ...), kind=kLoop, calls=%fused_computation.49 | loop fusion | flops 1835008 | bytes 1933312 | tf_op jit(solution)/shard_map/add | solution.py:88
  29.7 0.9 slice_bitcast_fusion.1
  30.7 1.7 %fusion.53 = f32[4,4,1,128]{3,2,1,0:T(1,128)S(1)} fusion(f32[4,4,128,128]{3,2,1,0:T(8,128)S(1)} %multiply_add_fusion.2, f32[4,4,128,1]{2,3,1,0:T(1,128)S(1)} %bitcast.272), kind=kOutput, calls=%fused_computation.114 | convolution fusion | flops 3145728 | bytes 1064960 | tf_op jit(solution)/shard_map/tpji,tpi->tpj/dot_general | solution.py:96
  32.4 4.2 %while.66 = (s32[]{:T(128)}, f32[4,128,128]{2,1,0:T(8,128)S(1)}, f32[3,4,128,128]{3,2,1,0:T(8,128)}, s32[]{:T(128)}) while((s32[]{:T(128)}, f32[4,128,128]{2,1,0:T(8,128)S(1)}, f32[3,4,128,128]{3,2,1,0:T(8,128)}, s32[]{:T(128)}) %tuple.113), condition=%wide.region_2.3_spmd, body=%wide.region_1.2_spmd.sunk | while | flops 100663296 | bytes 1310785 | solution.py:99
  32.5 1.3 fusion.117
  33.9 1.3 fusion.117
  35.3 1.3 fusion.117
  36.6 1.9 %collective-permute-start.1 = (f32[4,128,128]{2,1,0:T(8,128)S(1)}, f32[4,128,128]{2,1,0:T(8,128)}, u32[]{:S(2)}, u32[]{:S(2)}) collective-permute-start(f32[4,128,128]{2,1,0:T(8,128)S(1)} %get-tuple-element.137), channel_id=1, source_target_pairs={{0,2},{2,4},{4,6},{6,8},{8,10},{10,12},{12,14},{1,3},{3,5},{5,7},{... | collective-permute-start | bytes 786440 | tf_op jit(solution)/shard_map/ppermute | solution.py:17
  38.6 6.0 %while.70 = (s32[]{:T(128)}, f32[4,128]{1,0:T(4,128)S(1)}, f32[4,4,128,128]{3,2,1,0:T(8,128)}, f32[4,4,128]{2,1,0:T(4,128)S(1)}, s32[]{:T(128)}, /*index=5*/s32[]{:T(128)}) while((s32[]{:T(128)}, f32[4,128]{1,0:T(4,128)S(1)}, f32[4,4,128,128]{3,2,1,0:T(8,128)}, f32[4,4,128]{2,1,0:T(4,128)S(1)}, s32[]{:T(128)}, ...), condition=%wide.region_4.5_spmd.clone, body=%wide.region_3.4_spmd.clone.sunk | while | flops 787459 | bytes 276575 | solution.py:100
  38.6 1.5 fusion.129
  40.1 1.5 fusion.129
  41.6 1.5 fusion.129
  43.1 1.5 fusion.129
  44.5 1.9 %collective-permute-start.5 = (f32[4,128]{1,0:T(4,128)S(1)}, f32[4,128]{1,0:T(4,128)S(1)}, u32[]{:S(2)}, u32[]{:S(2)}) collective-permute-start(f32[4,128]{1,0:T(4,128)S(1)} %get-tuple-element.138), channel_id=1, source_target_pairs={{0,2},{2,4},{4,6},{6,8},{8,10},{10,12},{12,14},{1,3},{3,5},{5,7},{... | collective-permute-start | bytes 6152 | tf_op jit(solution)/shard_map/ppermute | solution.py:17
  46.5 1.5 collective-permute-done.1
  48.0 1.0 broadcast_select_fusion.3
  48.9 1.9 %collective-permute-start.2 = (f32[4,128,128]{2,1,0:T(8,128)S(1)}, f32[4,128,128]{2,1,0:T(8,128)}, u32[]{:S(2)}, u32[]{:S(2)}) collective-permute-start(f32[4,128,128]{2,1,0:T(8,128)S(1)} %broadcast_select_fusion.3), channel_id=1, source_target_pairs={{0,2},{2,4},{4,6},{6,8},{8,10},{10,12},{12,14},{1,3},{3,5},{5,7},{... | collective-permute-start | bytes 786440 | tf_op jit(solution)/shard_map/ppermute | solution.py:17
  50.9 1.9 %collective-permute-start.6 = (f32[4,128]{1,0:T(4,128)S(1)}, f32[4,128]{1,0:T(4,128)S(1)}, u32[]{:S(2)}, u32[]{:S(2)}) collective-permute-start(f32[4,128]{1,0:T(4,128)S(1)} %broadcast_select_fusion.5), channel_id=1, source_target_pairs={{0,2},{2,4},{4,6},{6,8},{8,10},{10,12},{12,14},{1,3},{3,5},{5,7},{... | collective-permute-start | bytes 6152 | tf_op jit(solution)/shard_map/ppermute | solution.py:17
  52.8 6.6 %collective-permute-done.6 = f32[4,128]{1,0:T(4,128)S(1)} collective-permute-done((f32[4,128]{1,0:T(4,128)S(1)}, f32[4,128]{1,0:T(4,128)S(1)}, u32[]{:S(2)}, u32[]{:S(2)}) %collective-permute-start.6) | collective-permute-done | bytes 2080 | tf_op jit(solution)/shard_map/ppermute | solution.py:17
  60.0 2.1 %convolution_select_fusion.5 = f32[4,128,128]{2,1,0:T(8,128)} fusion(f32[4,128,128]{2,1,0:T(8,128)S(1)} %broadcast_select_fusion.3, f32[4,128,128]{2,1,0:T(8,128)} %collective-permute-done.2, pred[]{:T(512)S(6)} %ge.14), kind=kOutput, calls=%fused_computation.43 | convolution fusion | flops 100728832 | bytes 786433 | tf_op jit(solution)/shard_map/pji,pik->pjk/dot_general | solution.py:21
  62.0 1.3 collective-permute-start.3
  63.3 1.3 collective-permute-start.7
  64.6 7.0 %collective-permute-done.7 = f32[4,128]{1,0:T(4,128)S(1)} collective-permute-done((f32[4,128]{1,0:T(4,128)S(1)}, f32[4,128]{1,0:T(4,128)S(1)}, u32[]{:S(2)}, u32[]{:S(2)}) %collective-permute-start.7) | collective-permute-done | bytes 2080 | tf_op jit(solution)/shard_map/ppermute | solution.py:17
  71.7 1.5 fusion.55
  73.1 2.1 %convolution_select_fusion.4 = f32[4,128,128]{2,1,0:T(8,128)} fusion(f32[4,128,128]{2,1,0:T(8,128)} %convolution_select_fusion.5, f32[4,128,128]{2,1,0:T(8,128)S(1)} %collective-permute-done.3, pred[]{:T(512)S(6)} %ge.13), kind=kOutput, calls=%fused_computation.42 | convolution fusion | flops 100728832 | bytes 786433 | tf_op jit(solution)/shard_map/pji,pik->pjk/dot_general | solution.py:21
  75.3 1.3 collective-permute-start.4
  76.6 1.3 collective-permute-start.8
  77.9 12.5 %collective-permute-done.8 = f32[4,128]{1,0:T(4,128)S(1)} collective-permute-done((f32[4,128]{1,0:T(4,128)S(1)}, f32[4,128]{1,0:T(4,128)S(1)}, u32[]{:S(2)}, u32[]{:S(2)}) %collective-permute-start.8) | collective-permute-done | bytes 2080 | tf_op jit(solution)/shard_map/ppermute | solution.py:17
  90.4 1.5 fusion.56
  91.9 1.5 convolution_select_fusion.3
  94.0 6.0 %while.67 = (s32[]{:T(128)}, f32[4,128]{1,0:T(4,128)S(1)}, f32[4,4,128]{2,1,0:T(4,128)S(1)}, f32[4,4,128,128]{3,2,1,0:T(8,128)}, f32[4,4,128]{2,1,0:T(4,128)S(1)}, /*index=5*/s32[]{:T(128)}) while((s32[]{:T(128)}, f32[4,128]{1,0:T(4,128)S(1)}, f32[4,4,128]{2,1,0:T(4,128)S(1)}, f32[4,4,128,128]{3,2,1,0:T(8,128)}, f32[4,4,128]{2,1,0:T(4,128)S(1)}, ...), condition=%wide.region_6.7_spmd, body=%wide.region_5.6_spmd.sunk | while | flops 786946 | bytes 274517 | solution.py:125
  94.0 1.5 fusion.120
  95.5 1.5 fusion.120
  96.9 1.5 fusion.120
  98.4 1.5 fusion.120
  100.0 2.0 %all_gather.7 = bf16[4,1024]{1,0:T(4,128)(2,1)S(1)} all-gather(bf16[4,512]{1,0:T(4,128)(2,1)S(1)} %pad_maximum_fusion.3), channel_id=1, replica_groups=mesh['sweep'=2,'tm'=8,'unit'=2] {'unit'}, dimensions={1}, use_global_device_ids=true | all-gather | bytes 12288 | tf_op jit(solution)/shard_map/all_gather | solution.py:68
  103.0 2.2 %multiply_add_fusion = f32[4,4,128,128]{3,2,1,0:T(8,128)S(1)} fusion(f32[4,4,128]{2,1,0:T(4,128)S(1)} %get-tuple-element.227, f32[4,4,128]{2,1,0:T(4,128)S(1)} %get-tuple-element.229, f32[4,4,128]{2,1,0:T(4,128)S(1)} %get-tuple-element.228, f32[4,4,128]{2,1,0:T(4,128)S(1)} %get-tuple-element.225, f32[128,128]{1,0:T(8,128)S(1)} %fusion.34, ...), kind=kLoop, calls=%fused_computation.46 | loop fusion | flops 1835008 | bytes 1933312 | tf_op jit(solution)/shard_map/add | solution.py:88
  105.2 2.2 %multiply_add_fusion.1 = f32[4,1,4,128,128]{4,3,2,0,1:T(8,128)S(1)} fusion(f32[4,4,128]{2,1,0:T(4,128)S(1)} %get-tuple-element.227, f32[4,4,128]{2,1,0:T(4,128)S(1)} %get-tuple-element.229, f32[4,4,128]{2,1,0:T(4,128)S(1)} %get-tuple-element.228, f32[4,4,128]{2,1,0:T(4,128)S(1)} %get-tuple-element.225, f32[128,128]{1,0:T(8,128)S(1)} %fusion.34, ...), kind=kLoop, calls=%fused_computation.47 | loop fusion | flops 1835008 | bytes 1933312 | tf_op jit(solution)/shard_map/add | solution.py:88
  107.5 1.7 %fusion.57 = f32[4,4,1,128]{3,2,1,0:T(1,128)S(1)} fusion(f32[4,4,128,128]{3,2,1,0:T(8,128)S(1)} %multiply_add_fusion, f32[4,4,128,1]{2,3,1,0:T(1,128)S(1)} %bitcast.271), kind=kOutput, calls=%fused_computation.118 | convolution fusion | flops 3145728 | bytes 1064960 | tf_op jit(solution)/shard_map/tpji,tpi->tpj/dot_general | solution.py:96
  109.2 1.3 while.68
  110.6 1.9 %collective-permute-start.9 = (f32[4,128,128]{2,1,0:T(8,128)S(1)}, f32[4,128,128]{2,1,0:T(8,128)S(1)}, u32[]{:S(2)}, u32[]{:S(2)}) collective-permute-start(f32[4,128,128]{2,1,0:T(8,128)S(1)} %get-tuple-element.140), channel_id=1, source_target_pairs={{0,2},{2,4},{4,6},{6,8},{8,10},{10,12},{12,14},{1,3},{3,5},{5,7},{... | collective-permute-start | bytes 786440 | tf_op jit(solution)/shard_map/ppermute | solution.py:17
  112.5 2.2 %while.71 = (s32[]{:T(128)}, f32[4,128]{1,0:T(4,128)S(1)}, f32[4,4,128,128]{3,2,1,0:T(8,128)S(1)}, f32[4,4,128]{2,1,0:T(4,128)S(1)}, s32[]{:T(128)}, /*index=5*/s32[]{:T(128)}) while((s32[]{:T(128)}, f32[4,128]{1,0:T(4,128)S(1)}, f32[4,4,128,128]{3,2,1,0:T(8,128)S(1)}, f32[4,4,128]{2,1,0:T(4,128)S(1)}, s32[]{:T(128)}, ...), condition=%wide.region_10.11_spmd.clone, body=%wide.region_9.10_spmd.clone.sunk | while | flops 787459 | bytes 276575 | solution.py:100
  114.7 1.9 %collective-permute-start.13 = (f32[4,128]{1,0:T(4,128)S(1)}, f32[4,128]{1,0:T(4,128)S(1)}, u32[]{:S(2)}, u32[]{:S(2)}) collective-permute-start(f32[4,128]{1,0:T(4,128)S(1)} %get-tuple-element.141), channel_id=1, source_target_pairs={{0,2},{2,4},{4,6},{6,8},{8,10},{10,12},{12,14},{1,3},{3,5},{5,7},{... | collective-permute-start | bytes 6152 | tf_op jit(solution)/shard_map/ppermute | solution.py:17
  116.6 5.2 %collective-permute-done.9 = f32[4,128,128]{2,1,0:T(8,128)S(1)} collective-permute-done((f32[4,128,128]{2,1,0:T(8,128)S(1)}, f32[4,128,128]{2,1,0:T(8,128)S(1)}, u32[]{:S(2)}, u32[]{:S(2)}) %collective-permute-start.9) | collective-permute-done | bytes 262176 | tf_op jit(solution)/shard_map/ppermute | solution.py:17
  121.8 1.9 %collective-permute-start.10 = (f32[4,128,128]{2,1,0:T(8,128)S(1)}, f32[4,128,128]{2,1,0:T(8,128)S(1)}, u32[]{:S(2)}, u32[]{:S(2)}) collective-permute-start(f32[4,128,128]{2,1,0:T(8,128)S(1)} %broadcast_select_fusion.2), channel_id=1, source_target_pairs={{0,2},{2,4},{4,6},{6,8},{8,10},{10,12},{12,14},{1,3},{3,5},{5,7},{... | collective-permute-start | bytes 786440 | tf_op jit(solution)/shard_map/ppermute | solution.py:17
  123.8 1.9 %collective-permute-start.14 = (f32[4,128]{1,0:T(4,128)S(1)}, f32[4,128]{1,0:T(4,128)S(1)}, u32[]{:S(2)}, u32[]{:S(2)}) collective-permute-start(f32[4,128]{1,0:T(4,128)S(1)} %broadcast_select_fusion.6), channel_id=1, source_target_pairs={{0,2},{2,4},{4,6},{6,8},{8,10},{10,12},{12,14},{1,3},{3,5},{5,7},{... | collective-permute-start | bytes 6152 | tf_op jit(solution)/shard_map/ppermute | solution.py:17
  125.7 6.5 %collective-permute-done.14 = f32[4,128]{1,0:T(4,128)S(1)} collective-permute-done((f32[4,128]{1,0:T(4,128)S(1)}, f32[4,128]{1,0:T(4,128)S(1)}, u32[]{:S(2)}, u32[]{:S(2)}) %collective-permute-start.14) | collective-permute-done | bytes 2080 | tf_op jit(solution)/shard_map/ppermute | solution.py:17
  133.2 1.3 collective-permute-start.11
  134.5 1.3 collective-permute-start.15
  135.8 6.0 %collective-permute-done.15 = f32[4,128]{1,0:T(4,128)S(1)} collective-permute-done((f32[4,128]{1,0:T(4,128)S(1)}, f32[4,128]{1,0:T(4,128)S(1)}, u32[]{:S(2)}, u32[]{:S(2)}) %collective-permute-start.15) | collective-permute-done | bytes 2080 | tf_op jit(solution)/shard_map/ppermute | solution.py:17
  142.7 1.3 collective-permute-start.12
  144.0 1.3 collective-permute-start.16
  145.3 11.6 %collective-permute-done.16 = f32[4,128]{1,0:T(4,128)S(1)} collective-permute-done((f32[4,128]{1,0:T(4,128)S(1)}, f32[4,128]{1,0:T(4,128)S(1)}, u32[]{:S(2)}, u32[]{:S(2)}) %collective-permute-start.16) | collective-permute-done | bytes 2080 | tf_op jit(solution)/shard_map/ppermute | solution.py:17
  158.4 2.2 %while.69 = (s32[]{:T(128)}, f32[4,128]{1,0:T(4,128)S(1)}, f32[4,4,128]{2,1,0:T(4,128)S(1)}, f32[4,4,128,128]{3,2,1,0:T(8,128)S(1)}, f32[4,4,128]{2,1,0:T(4,128)S(1)}, /*index=5*/s32[]{:T(128)}) while((s32[]{:T(128)}, f32[4,128]{1,0:T(4,128)S(1)}, f32[4,4,128]{2,1,0:T(4,128)S(1)}, f32[4,4,128,128]{3,2,1,0:T(8,128)S(1)}, ...), condition=%wide.region_12.13_spmd, body=%wide.region_11.12_spmd.sunk | while | flops 786946 | bytes 274517 | solution.py:125
  (124 shorter events, 16.1 us)
Async XLA Ops:
  0.7 21.4 %collective-permute-start = (f32[1,512]{1,0:T(1,128)S(1)}, f32[1,512]{1,0:T(1,128)S(1)}, u32[]{:S(2)}, u32[]{:S(2)}) collective-permute-start(f32[1,512]{1,0:T(1,128)S(1)} %slice_bitcast_fusion.7), channel_id=1, source_target_pairs={{0,2},{2,4},{4,6},{6,8},{8,10},{10,12},{12,14},{1,3},{3,5},{5,7},{... | collective-permute-start | bytes 6152 | tf_op jit(solution)/shard_map/ppermute | solution.py:17
  14.0 3.3 %copy-start.5 = (f32[1,4,512]{2,1,0:T(4,128)S(1)}, f32[1,4,512]{2,1,0:T(4,128)}, u32[]{:S(2)}) copy-start(f32[1,4,512]{2,1,0:T(4,128)} %param.23) | copy-start | bytes 24580
  14.0 8.1 %copy-start.6 = (f32[1,512]{1,0:T(1,128)S(1)}, f32[1,512]{1,0:T(1,128)}, u32[]{:S(2)}) copy-start(f32[1,512]{1,0:T(1,128)} %param.22) | copy-start | bytes 6148
  17.2 7.6 %copy-start.3 = (bf16[1,4,3,512]{3,1,2,0:T(4,128)(2,1)S(1)}, bf16[1,4,3,512]{3,1,2,0:T(4,128)(2,1)}, u32[]{:S(2)}) copy-start(bf16[1,4,3,512]{3,1,2,0:T(4,128)(2,1)} %param.18) | copy-start | bytes 36868
  17.2 7.7 %copy-start.4 = (f32[512]{0:T(512)S(1)}, f32[512]{0:T(512)}, u32[]{:S(2)}) copy-start(f32[512]{0:T(512)} %param.21) | copy-start | bytes 6148
  17.2 7.7 %copy-start.7 = (f32[512]{0:T(512)S(1)}, f32[512]{0:T(512)}, u32[]{:S(2)}) copy-start(f32[512]{0:T(512)} %param.20) | copy-start | bytes 6148
  18.4 8.8 %copy-start.1 = (f32[4,128,128]{2,1,0:T(8,128)}, f32[4,128,128]{2,1,0:T(8,128)S(1)}, u32[]{:S(2)}) copy-start(f32[4,128,128]{2,1,0:T(8,128)S(1)} %copy.9) | copy-start | bytes 786436
  27.1 3.5 %copy-start = (f32[4,4,128,128]{3,2,1,0:T(8,128)}, f32[4,4,128,128]{3,2,1,0:T(8,128)S(1)}, u32[]{:S(2)}) copy-start(f32[4,4,128,128]{3,2,1,0:T(8,128)S(1)} %multiply_add_fusion.2) | copy-start | bytes 3145732
  36.6 11.3 %collective-permute-start.1 = (f32[4,128,128]{2,1,0:T(8,128)S(1)}, f32[4,128,128]{2,1,0:T(8,128)}, u32[]{:S(2)}, u32[]{:S(2)}) collective-permute-start(f32[4,128,128]{2,1,0:T(8,128)S(1)} %get-tuple-element.137), channel_id=1, source_target_pairs={{0,2},{2,4},{4,6},{6,8},{8,10},{10,12},{12,14},{1,3},{3,5},{5,7},{... | collective-permute-start | bytes 786440 | tf_op jit(solution)/shard_map/ppermute | solution.py:17
  44.5 6.4 %collective-permute-start.5 = (f32[4,128]{1,0:T(4,128)S(1)}, f32[4,128]{1,0:T(4,128)S(1)}, u32[]{:S(2)}, u32[]{:S(2)}) collective-permute-start(f32[4,128]{1,0:T(4,128)S(1)} %get-tuple-element.138), channel_id=1, source_target_pairs={{0,2},{2,4},{4,6},{6,8},{8,10},{10,12},{12,14},{1,3},{3,5},{5,7},{... | collective-permute-start | bytes 6152 | tf_op jit(solution)/shard_map/ppermute | solution.py:17
  48.9 11.0 %collective-permute-start.2 = (f32[4,128,128]{2,1,0:T(8,128)S(1)}, f32[4,128,128]{2,1,0:T(8,128)}, u32[]{:S(2)}, u32[]{:S(2)}) collective-permute-start(f32[4,128,128]{2,1,0:T(8,128)S(1)} %broadcast_select_fusion.3), channel_id=1, source_target_pairs={{0,2},{2,4},{4,6},{6,8},{8,10},{10,12},{12,14},{1,3},{3,5},{5,7},{... | collective-permute-start | bytes 786440 | tf_op jit(solution)/shard_map/ppermute | solution.py:17
  50.9 8.5 %collective-permute-start.6 = (f32[4,128]{1,0:T(4,128)S(1)}, f32[4,128]{1,0:T(4,128)S(1)}, u32[]{:S(2)}, u32[]{:S(2)}) collective-permute-start(f32[4,128]{1,0:T(4,128)S(1)} %broadcast_select_fusion.5), channel_id=1, source_target_pairs={{0,2},{2,4},{4,6},{6,8},{8,10},{10,12},{12,14},{1,3},{3,5},{5,7},{... | collective-permute-start | bytes 6152 | tf_op jit(solution)/shard_map/ppermute | solution.py:17
  62.0 11.1 %collective-permute-start.3 = (f32[4,128,128]{2,1,0:T(8,128)}, f32[4,128,128]{2,1,0:T(8,128)S(1)}, u32[]{:S(2)}, u32[]{:S(2)}) collective-permute-start(f32[4,128,128]{2,1,0:T(8,128)} %convolution_select_fusion.5), channel_id=1, source_target_pairs={{0,4},{2,6},{4,8},{6,10},{8,12},{10,14},{1,5},{3,7},{5,9},{7,11},{... | collective-permute-start | bytes 786440 | tf_op jit(solution)/shard_map/ppermute | solution.py:17
  63.3 8.3 %collective-permute-start.7 = (f32[4,128]{1,0:T(4,128)S(1)}, f32[4,128]{1,0:T(4,128)S(1)}, u32[]{:S(2)}, u32[]{:S(2)}) collective-permute-start(f32[4,128]{1,0:T(4,128)S(1)} %add_select_fusion.5), channel_id=1, source_target_pairs={{0,4},{2,6},{4,8},{6,10},{8,12},{10,14},{1,5},{3,7},{5,9},{7,11},{... | collective-permute-start | bytes 6152 | tf_op jit(solution)/shard_map/ppermute | solution.py:17
  75.3 16.6 %collective-permute-start.4 = (f32[4,128,128]{2,1,0:T(8,128)}, f32[4,128,128]{2,1,0:T(8,128)}, u32[]{:S(2)}, u32[]{:S(2)}) collective-permute-start(f32[4,128,128]{2,1,0:T(8,128)} %convolution_select_fusion.4), channel_id=1, source_target_pairs={{0,8},{2,10},{4,12},{6,14},{1,9},{3,11},{5,13},{7,15},{16,24},{18,... | collective-permute-start | bytes 786440 | tf_op jit(solution)/shard_map/ppermute | solution.py:17
  76.6 13.8 %collective-permute-start.8 = (f32[4,128]{1,0:T(4,128)S(1)}, f32[4,128]{1,0:T(4,128)S(1)}, u32[]{:S(2)}, u32[]{:S(2)}) collective-permute-start(f32[4,128]{1,0:T(4,128)S(1)} %add_select_fusion.4), channel_id=1, source_target_pairs={{0,8},{2,10},{4,12},{6,14},{1,9},{3,11},{5,13},{7,15},{16,24},{18,... | collective-permute-start | bytes 6152 | tf_op jit(solution)/shard_map/ppermute | solution.py:17
  90.4 12.6 %copy-start.2 = (f32[4,128,128]{2,1,0:T(8,128)S(1)}, f32[4,128,128]{2,1,0:T(8,128)}, u32[]{:S(2)}) copy-start(f32[4,128,128]{2,1,0:T(8,128)} %copy-done.1) | copy-start | bytes 786436
  110.6 11.2 %collective-permute-start.9 = (f32[4,128,128]{2,1,0:T(8,128)S(1)}, f32[4,128,128]{2,1,0:T(8,128)S(1)}, u32[]{:S(2)}, u32[]{:S(2)}) collective-permute-start(f32[4,128,128]{2,1,0:T(8,128)S(1)} %get-tuple-element.140), channel_id=1, source_target_pairs={{0,2},{2,4},{4,6},{6,8},{8,10},{10,12},{12,14},{1,3},{3,5},{5,7},{... | collective-permute-start | bytes 786440 | tf_op jit(solution)/shard_map/ppermute | solution.py:17
  114.7 9.1 %collective-permute-start.13 = (f32[4,128]{1,0:T(4,128)S(1)}, f32[4,128]{1,0:T(4,128)S(1)}, u32[]{:S(2)}, u32[]{:S(2)}) collective-permute-start(f32[4,128]{1,0:T(4,128)S(1)} %get-tuple-element.141), channel_id=1, source_target_pairs={{0,2},{2,4},{4,6},{6,8},{8,10},{10,12},{12,14},{1,3},{3,5},{5,7},{... | collective-permute-start | bytes 6152 | tf_op jit(solution)/shard_map/ppermute | solution.py:17
  121.8 10.9 %collective-permute-start.10 = (f32[4,128,128]{2,1,0:T(8,128)S(1)}, f32[4,128,128]{2,1,0:T(8,128)S(1)}, u32[]{:S(2)}, u32[]{:S(2)}) collective-permute-start(f32[4,128,128]{2,1,0:T(8,128)S(1)} %broadcast_select_fusion.2), channel_id=1, source_target_pairs={{0,2},{2,4},{4,6},{6,8},{8,10},{10,12},{12,14},{1,3},{3,5},{5,7},{... | collective-permute-start | bytes 786440 | tf_op jit(solution)/shard_map/ppermute | solution.py:17
  123.8 8.5 %collective-permute-start.14 = (f32[4,128]{1,0:T(4,128)S(1)}, f32[4,128]{1,0:T(4,128)S(1)}, u32[]{:S(2)}, u32[]{:S(2)}) collective-permute-start(f32[4,128]{1,0:T(4,128)S(1)} %broadcast_select_fusion.6), channel_id=1, source_target_pairs={{0,2},{2,4},{4,6},{6,8},{8,10},{10,12},{12,14},{1,3},{3,5},{5,7},{... | collective-permute-start | bytes 6152 | tf_op jit(solution)/shard_map/ppermute | solution.py:17
  133.2 9.1 %collective-permute-start.11 = (f32[4,128,128]{2,1,0:T(8,128)S(1)}, f32[4,128,128]{2,1,0:T(8,128)S(1)}, u32[]{:S(2)}, u32[]{:S(2)}) collective-permute-start(f32[4,128,128]{2,1,0:T(8,128)S(1)} %convolution_select_fusion.2), channel_id=1, source_target_pairs={{0,4},{2,6},{4,8},{6,10},{8,12},{10,14},{1,5},{3,7},{5,9},{7,11},{... | collective-permute-start | bytes 786440 | tf_op jit(solution)/shard_map/ppermute | solution.py:17
  134.5 7.3 %collective-permute-start.15 = (f32[4,128]{1,0:T(4,128)S(1)}, f32[4,128]{1,0:T(4,128)S(1)}, u32[]{:S(2)}, u32[]{:S(2)}) collective-permute-start(f32[4,128]{1,0:T(4,128)S(1)} %add_select_fusion.2), channel_id=1, source_target_pairs={{0,4},{2,6},{4,8},{6,10},{8,12},{10,14},{1,5},{3,7},{5,9},{7,11},{... | collective-permute-start | bytes 6152 | tf_op jit(solution)/shard_map/ppermute | solution.py:17
  142.7 14.7 %collective-permute-start.12 = (f32[4,128,128]{2,1,0:T(8,128)S(1)}, f32[4,128,128]{2,1,0:T(8,128)S(1)}, u32[]{:S(2)}, u32[]{:S(2)}) collective-permute-start(f32[4,128,128]{2,1,0:T(8,128)S(1)} %convolution_select_fusion.1), channel_id=1, source_target_pairs={{0,8},{2,10},{4,12},{6,14},{1,9},{3,11},{5,13},{7,15},{16,24},{18,... | collective-permute-start | bytes 786440 | tf_op jit(solution)/shard_map/ppermute | solution.py:17
  144.0 12.9 %collective-permute-start.16 = (f32[4,128]{1,0:T(4,128)S(1)}, f32[4,128]{1,0:T(4,128)S(1)}, u32[]{:S(2)}, u32[]{:S(2)}) collective-permute-start(f32[4,128]{1,0:T(4,128)S(1)} %add_select_fusion.1), channel_id=1, source_target_pairs={{0,8},{2,10},{4,12},{6,14},{1,9},{3,11},{5,13},{7,15},{16,24},{18,... | collective-permute-start | bytes 6152 | tf_op jit(solution)/shard_map/ppermute | solution.py:17
where the time goes:
time: 163 us; the launch traced here: 161 us
  waiting for transfers between devices  57 us (35%)
  matrix products  39.3 us (24%)
  starting transfers between devices  29.1 us (18%)
  other arithmetic  15.6 us (10%)
  local copies, waits for them, and re-layouts  15.4 us (9%)
  blocking collectives  3.77 us (2%)
    ppermute x17, waiting for transfers between devices, passed_along(): lax.ppermute(value, axis, [(source, source + steps) for source in range(i...  57 us
    ppermute x17, starting transfers between devices, passed_along(): lax.ppermute(value, axis, [(source, source + steps) for source in range(i...  29.1 us
    dot_general x18, matrix products, apply_map(): jnp.einsum('pji,pi->pj', matrix, current, precision=HIGHEST_MODE) + vector  16.9 us
    add x4, other arithmetic, shards(): coef_a[..., None] * diagonal[0] + coef_c[..., None] * diagonal[1]  9.08 us
    dot_general x6, matrix products, combine(): jnp.einsum('pji,pik->pjk', later[0], earlier[0], precision=HIGHEST_MODE)  6.96 us
    dot_general x6, matrix products, compose(): jnp.einsum('pji,pik->pjk', jac_step, product, precision=HIGHEST_MODE)  5.22 us
    dot_general x6, matrix products, combine(): jnp.einsum('pji,pi->pj', later[0], earlier[1], precision=HIGHEST_MODE)  4.98 us
    all_gather x2, blocking collectives, shards(): lax.all_gather(panels, 'unit', axis=1, tiled=True)  3.77 us
  transfers between devices with their start and end apart: 17, of which 9 were waited for; matrix products, arithmetic and copies ran while one was open for 20% of the time, Pallas kernels for 0%

commit v1 on v0

v1 whole, which is shorter than its diff:
```python
import functools

import jax
import jax.numpy as jnp
from jax import lax
from jax.experimental import pallas as pl
from jax.experimental.pallas import tpu as pltpu
from jax.sharding import PartitionSpec as P

BLOCK = 128
NEWTON = 2
GROUP = 8
COEFS = 5
FINE = (0, 4)
SENT = COEFS + len(FINE)
MESH = pl.DeviceIdType.MESH


def to(tm, unit):
    return {"tm": tm, "unit": unit}


def newton_kernel(
    n_tm, n_unit, proj, w_hbm, bias_u, bias_c, start, guess_in, out,
    w_all, w_diag, stage, mates, nears, own, packed, coefs, moves, relay_out, relay_in,
    w_sem, mate_send, mate_recv, near_send, near_recv, coef_send, coef_recv, relay_send, relay_recv,
):
    steps, width = guess_in.shape
    blocks = width // BLOCK
    rows = steps * blocks
    group = min(GROUP, n_tm)
    n_groups = n_tm // group
    time = lax.axis_index("tm")
    unit = lax.axis_index("unit")
    place = lax.rem(time, group)
    reach = min(n_tm - 1, group if n_groups > 1 else group - 1)

    loads = [
        pltpu.make_async_copy(w_hbm.at[gate], w_all.at[gate], w_sem.at[gate]) for gate in range(3)
    ]
    for load in loads:
        load.start()

    barrier = pltpu.get_barrier_semaphore()
    greeted = jnp.int32(n_unit - 1)
    for away in range(1, n_unit):
        pl.semaphore_signal(
            barrier, inc=1, device_id=to(time, lax.rem(unit + away, n_unit)), device_id_type=MESH
        )
    for away in range(1, reach + 1):
        turns = range(n_unit if away == 1 else 1)
        for there, valid in ((time + away, time + away < n_tm), (time - away, time >= away)):
            greeted = greeted + jnp.where(valid, len(turns), 0)

            @pl.when(valid)
            def _():
                for turn in turns:
                    pl.semaphore_signal(
                        barrier, inc=1, device_id=to(there, lax.rem(unit + turn, n_unit)), device_id_type=MESH
                    )

    stage[0, 0:steps, :] = guess_in[...]
    stage[0, steps : steps + 1, :] = start[...]
    pl.semaphore_wait(barrier, greeted)

    def mate_copy(turn, away):
        return pltpu.make_async_remote_copy(
            src_ref=stage.at[turn], dst_ref=mates.at[turn, away - 1],
            send_sem=mate_send.at[turn, away - 1], recv_sem=mate_recv.at[turn, away - 1],
            device_id=to(time, lax.rem(unit + away, n_unit)), device_id_type=MESH,
        )

    def near_copy(away):
        return pltpu.make_async_remote_copy(
            src_ref=stage.at[0], dst_ref=nears.at[away],
            send_sem=near_send.at[away], recv_sem=near_recv.at[away],
            device_id=to(lax.rem(time + 1, n_tm), lax.rem(unit + away, n_unit)), device_id_type=MESH,
        )

    def coef_copy(turn, away):
        return pltpu.make_async_remote_copy(
            src_ref=packed.at[turn], dst_ref=coefs.at[turn, away - 1],
            send_sem=coef_send.at[turn, away - 1], recv_sem=coef_recv.at[turn, away - 1],
            device_id=to(lax.rem(time + away, n_tm), unit), device_id_type=MESH,
        )

    def relay_copy(turn, target):
        return pltpu.make_async_remote_copy(
            src_ref=relay_out.at[turn], dst_ref=relay_in.at[turn],
            send_sem=relay_send.at[turn, target], recv_sem=relay_recv.at[turn],
            device_id=to(lax.rem(time + 1 + target, n_tm), unit), device_id_type=MESH,
        )

    for away in range(1, n_unit):
        mate_copy(0, away).start()

    @pl.when(time < n_tm - 1)
    def _():
        for away in range(n_unit):
            near_copy(away).start()

    @pl.when(time > 0)
    def _():
        for away in range(n_unit):
            near_copy(away).wait_recv()

    def entering_from(held, away):
        return jnp.where(time == 0, held[steps : steps + 1, :], nears[(n_unit - away) % n_unit, steps - 1 : steps, :])

    guess = guess_in[...]
    previous = jnp.concatenate([entering_from(stage[0], 0), guess[: steps - 1]], axis=0)
    row = lax.broadcasted_iota(jnp.int32, (16, BLOCK), 0) % 8

    for turn in range(NEWTON):
        if turn:
            stage[turn, 0:steps, :] = previous
            for away in range(1, n_unit):
                mate_copy(turn, away).start()

        if turn == 0:
            for load in loads:
                load.wait()
            for block in range(blocks):
                first = pl.multiple_of(unit * width + block * BLOCK, BLOCK)
                here = slice(block * BLOCK, (block + 1) * BLOCK)
                for gate in range(3):
                    w_diag[here, gate * BLOCK : (gate + 1) * BLOCK] = w_all[gate, pl.ds(first, BLOCK), here]

        def product(panel, owner):
            first = pl.multiple_of(owner * width, width)
            panel = jnp.concatenate([panel] * (16 // steps), axis=0).astype(jnp.bfloat16)
            return [
                jnp.dot(panel, w_all[gate, pl.ds(first, width), :], preferred_element_type=jnp.float32)[:steps]
                for gate in range(3)
            ]

        rec = product(previous, unit)
        for away in range(1, n_unit):
            mate_copy(turn, away).wait_recv()
            held = mates[turn, away - 1]
            if turn:
                panel = held[:steps]
            else:
                panel = jnp.concatenate([entering_from(held, n_unit - away), held[: steps - 1]], axis=0)
            rec = [x + y for x, y in zip(rec, product(panel, lax.rem(unit + n_unit - away, n_unit)))]

        update_in = proj[0].astype(jnp.float32) + rec[0] + bias_u[...]
        update = jax.nn.sigmoid(update_in)
        fresh = jax.nn.sigmoid(-update_in)
        reset = jax.nn.sigmoid(proj[1].astype(jnp.float32) + rec[1])
        cand_rec = rec[2] + bias_c[...]
        cand = jnp.tanh(proj[2].astype(jnp.float32) + reset * cand_rec)
        coef_d = fresh * (1.0 - cand * cand) * reset
        values = (
            fresh,
            (previous - cand) * update * fresh,
            coef_d * cand_rec * (1.0 - reset),
            coef_d,
            fresh * cand + update * previous - guess,
        )
        for index, value in enumerate(values):
            for block in range(blocks):
                own[index, pl.ds(block, steps, stride=blocks), :] = value[:, block * BLOCK : (block + 1) * BLOCK]
        packed[turn, 0:COEFS] = own[...].astype(jnp.bfloat16)
        for slot, index in enumerate(FINE):
            full = own[index]
            packed[turn, COEFS + slot] = (full - full.astype(jnp.bfloat16).astype(jnp.float32)).astype(jnp.bfloat16)

        for away in range(group - 1, 0, -1):
            @pl.when(place + away < group)
            def _():
                coef_copy(turn, away).start()

        def step(delta, five):
            high = delta.astype(jnp.bfloat16).astype(jnp.float32)
            both = jnp.concatenate([high, delta - high], axis=0)
            left = jnp.concatenate(
                [jnp.where(row == block, both, 0.0) for block in range(blocks)], axis=1
            ).astype(jnp.bfloat16)
            terms = jnp.dot(left, w_diag[...], preferred_element_type=jnp.float32)
            terms = terms[:8] + terms[8:]
            fresh, a, c, d, gap = five
            return (
                (gap + delta - fresh * delta) + a * terms[:, :BLOCK]
                + c * terms[:, BLOCK : 2 * BLOCK] + d * terms[:, 2 * BLOCK :]
            )

        def at_step(table, t):
            def pick(value):
                part = value[t * blocks : (t + 1) * blocks]
                return jnp.concatenate([part] * (8 // blocks), axis=0)

            return [pick(table[index]) for index in range(COEFS)]

        def pass_block(source, delta):
            away = place - source
            slot = away - 1
            pltpu.make_async_remote_copy(
                src_ref=packed.at[turn], dst_ref=coefs.at[turn, slot],
                send_sem=coef_send.at[turn, slot], recv_sem=coef_recv.at[turn, slot],
                device_id=to(lax.rem(time + 1, n_tm), unit), device_id_type=MESH,
            ).wait_recv()
            table = [coefs[turn, slot, index].astype(jnp.float32) for index in range(SENT)]
            for low, index in enumerate(FINE):
                table[index] = table[index] + table[COEFS + low]
            for t in range(steps):
                delta = step(delta, at_step(table, t))
            return delta

        delta = jnp.zeros((8, BLOCK), jnp.float32)
        if n_groups > 1:
            relay_in_now = relay_in.at[turn]

            @pl.when(time < group)
            def _():
                relay_in_now[...] = jnp.zeros((8, BLOCK), jnp.float32)

            @pl.when(time >= group)
            def _():
                relay_copy(turn, 0).wait_recv()

            delta = relay_in_now[...]
        delta = lax.fori_loop(0, place, pass_block, delta)
        moves[0:blocks, :] = delta[:blocks]
        table = own[...]
        for t in range(steps):
            delta = step(delta, at_step(table, t))
            moves[(t + 1) * blocks : (t + 2) * blocks, :] = delta[:blocks]
        if n_groups > 1:
            relay_out[turn] = delta

            @pl.when((place == group - 1) & (time < n_tm - 1))
            def _():
                for target in range(group):
                    relay_copy(turn, target).start()

        def moved(skip):
            return jnp.concatenate(
                [moves[pl.ds(skip * blocks + block, steps, stride=blocks), :] for block in range(blocks)], axis=1
            )

        guess = guess + moved(1)
        if turn < NEWTON - 1:
            previous = previous + moved(0)
    out[...] = guess

    @pl.when(time < n_tm - 1)
    def _():
        for away in range(n_unit):
            near_copy(away).wait_send()

    for turn in range(NEWTON):
        for away in range(1, n_unit):
            mate_copy(turn, away).wait_send()
        for away in range(1, group):
            @pl.when(place + away < group)
            def _():
                coef_copy(turn, away).wait_send()
        if n_groups > 1:
            @pl.when((place == group - 1) & (time < n_tm - 1))
            def _():
                for target in range(group):
                    relay_copy(turn, target).wait_send()


def shards(n_tm, n_unit, projections, recurrent, update_bias, candidate_bias, start_state, initial_guess):
    _, steps, _, width = projections.shape
    full = recurrent.shape[0]
    rows = steps * (width // BLOCK)
    group = min(GROUP, n_tm)
    vmem = pl.BlockSpec(memory_space=pltpu.VMEM)
    f32, bf16 = jnp.float32, jnp.bfloat16
    held = 8 * pl.cdiv(steps + 1, 8)
    dma = pltpu.SemaphoreType.DMA
    result = pl.pallas_call(
        functools.partial(newton_kernel, n_tm, n_unit),
        out_shape=jax.ShapeDtypeStruct((steps, width), f32),
        in_specs=[vmem, pl.BlockSpec(memory_space=pl.ANY), vmem, vmem, vmem, vmem],
        out_specs=vmem,
        scratch_shapes=[
            pltpu.VMEM((3, full, width), bf16),
            pltpu.VMEM((width, 3 * BLOCK), bf16),
            pltpu.VMEM((NEWTON, held, width), f32),
            pltpu.VMEM((NEWTON, n_unit - 1, held, width), f32),
            pltpu.VMEM((n_unit, held, width), f32),
            pltpu.VMEM((COEFS, rows, BLOCK), f32),
            pltpu.VMEM((NEWTON, SENT, rows, BLOCK), bf16),
            pltpu.VMEM((NEWTON, group - 1, SENT, rows, BLOCK), bf16),
            pltpu.VMEM((rows + 8, BLOCK), f32),
            pltpu.VMEM((NEWTON, 8, BLOCK), f32),
            pltpu.VMEM((NEWTON, 8, BLOCK), f32),
            dma((3,)),
            dma((NEWTON, n_unit - 1)),
            dma((NEWTON, n_unit - 1)),
            dma((n_unit,)),
            dma((n_unit,)),
            dma((NEWTON, group - 1)),
            dma((NEWTON, group - 1)),
            dma((NEWTON, group)),
            dma((NEWTON,)),
        ],
        compiler_params=pltpu.CompilerParams(
            collective_id=0, has_side_effects=True, vmem_limit_bytes=32 * 1024 * 1024
        ),
        name="newton",
    )(
        jnp.transpose(projections[0], (1, 0, 2)),
        jnp.transpose(recurrent, (1, 0, 2)),
        update_bias.reshape(1, width),
        candidate_bias.reshape(1, width),
        start_state,
        initial_guess[0],
    )
    return result[None]


def solution(mesh):
    return jax.shard_map(
        functools.partial(shards, mesh.shape["tm"], mesh.shape["unit"]),
        mesh=mesh,
        in_specs=(
            P("sweep", "tm", None, "unit"),
            P("sweep", None, "unit"),
            P(("sweep", "unit")),
            P(("sweep", "unit")),
            P("sweep", "unit"),
            P("sweep", "tm", "unit"),
        ),
        out_specs=P("sweep", "tm", "unit"),
        check_vma=False,
    )
```

time: 163 us -> 30.6 us (0.19)
  the two profiles are of different devices: /device:TPU:24 before, /device:TPU:31 now
where the time goes in v1:
time: 30.6 us; the launch traced here: 30.2 us
  Pallas kernels  24.2 us (79%)
  local copies, waits for them, and re-layouts  5.94 us (19%)
    pallas_call x1, Pallas kernels, shards(): pl.pallas_call(functools.partial(newton_kernel, n_tm, n_unit), out_shape=...  24.2 us
    unnamed x13, local copies, waits for them, and re-layouts  5.94 us

profile of v1, /device:TPU:31, one launch (start us, length us, event | category | flops | bytes accessed | tf_op | source)
XLA Modules:
  0.0 30.2 jit_solution(7410374229312800120)
XLA Ops:
  0.0 0.0 copy-start
  0.0 1.9 %copy-done = bf16[1024,3,512]{2,0,1:T(8,128)(2,1)S(1)} copy-done((bf16[1024,3,512]{2,0,1:T(8,128)(2,1)S(1)}, bf16[1024,3,512]{2,0,1:T(8,128)(2,1)}, u32[]{:S(2)}) %copy-start) | copy-done | bytes 3145752
  1.9 0.0 copy-start.1
  1.9 0.7 %copy-done.1 = bf16[1,4,3,512]{3,1,2,0:T(4,128)(2,1)S(1)} copy-done((bf16[1,4,3,512]{3,1,2,0:T(4,128)(2,1)S(1)}, bf16[1,4,3,512]{3,1,2,0:T(4,128)(2,1)}, u32[]{:S(2)}) %copy-start.1) | copy-done | bytes 12312
  2.6 0.0 copy-start.2
  2.6 0.7 %copy-done.2 = f32[1,4,512]{2,1,0:T(4,128)S(1)} copy-done((f32[1,4,512]{2,1,0:T(4,128)S(1)}, f32[1,4,512]{2,1,0:T(4,128)}, u32[]{:S(2)}) %copy-start.2) | copy-done | bytes 8216
  3.3 0.0 copy-start.3
  3.3 0.7 %copy-done.3 = f32[512]{0:T(512)S(1)} copy-done((f32[512]{0:T(512)S(1)}, f32[512]{0:T(512)}, u32[]{:S(2)}) %copy-start.3) | copy-done | bytes 2072
  4.0 0.0 copy-start.4
  4.0 0.7 %copy-done.4 = f32[512]{0:T(512)S(1)} copy-done((f32[512]{0:T(512)S(1)}, f32[512]{0:T(512)}, u32[]{:S(2)}) %copy-start.4) | copy-done | bytes 2072
  4.7 0.0 copy-start.5
  4.7 0.7 %copy-done.5 = f32[1,512]{1,0:T(1,128)S(1)} copy-done((f32[1,512]{1,0:T(1,128)S(1)}, f32[1,512]{1,0:T(1,128)}, u32[]{:S(2)}) %copy-start.5) | copy-done | bytes 2072
  5.3 24.2 %newton.1 = f32[4,512]{1,0:T(4,128)S(1)} custom-call(bf16[3,4,512]{2,1,0:T(4,128)(2,1)S(1)} %bitcast.10, bf16[3,1024,512]{2,1,0:T(8,128)(2,1)S(1)} %bitcast.8, f32[1,512]{1,0:T(1,128)S(1)} %bitcast.12, f32[1,512]{1,0:T(1,128)S(1)} %bitcast.13, f32[1,512]{1,0:T(1,128)S(1)} %copy-done.5, f32[4,512]{1,0:T(4,128)S(1)} %bitcast.11), custom_call_target="tpu_custom_call" | custom-call | tf_op jit(solution)/shard_map/newton/pallas_call | solution.py:275
  29.6 0.6 %copy.8 = f32[1,4,512]{2,1,0:T(4,128)} copy(f32[1,4,512]{2,1,0:T(4,128)S(1)} %bitcast.9) | data formatting | bytes 16384
Async XLA Ops:
  0.0 1.9 %copy-start = (bf16[1024,3,512]{2,0,1:T(8,128)(2,1)S(1)}, bf16[1024,3,512]{2,0,1:T(8,128)(2,1)}, u32[]{:S(2)}) copy-start(bf16[1024,3,512]{2,0,1:T(8,128)(2,1)} %param.7) | copy-start | bytes 9437188
  1.9 0.7 %copy-start.1 = (bf16[1,4,3,512]{3,1,2,0:T(4,128)(2,1)S(1)}, bf16[1,4,3,512]{3,1,2,0:T(4,128)(2,1)}, u32[]{:S(2)}) copy-start(bf16[1,4,3,512]{3,1,2,0:T(4,128)(2,1)} %param.6) | copy-start | bytes 36868
  2.6 0.7 %copy-start.2 = (f32[1,4,512]{2,1,0:T(4,128)S(1)}, f32[1,4,512]{2,1,0:T(4,128)}, u32[]{:S(2)}) copy-start(f32[1,4,512]{2,1,0:T(4,128)} %param.11) | copy-start | bytes 24580
  3.3 0.7 %copy-start.3 = (f32[512]{0:T(512)S(1)}, f32[512]{0:T(512)}, u32[]{:S(2)}) copy-start(f32[512]{0:T(512)} %param.8) | copy-start | bytes 6148
  4.0 0.7 %copy-start.4 = (f32[512]{0:T(512)S(1)}, f32[512]{0:T(512)}, u32[]{:S(2)}) copy-start(f32[512]{0:T(512)} %param.9) | copy-start | bytes 6148
  4.7 0.7 %copy-start.5 = (f32[1,512]{1,0:T(1,128)S(1)}, f32[1,512]{1,0:T(1,128)}, u32[]{:S(2)}) copy-start(f32[1,512]{1,0:T(1,128)} %start.1) | copy-start | bytes 6148

commit v2 on v1

--- a/solution.py
+++ b/solution.py
@@ -21,11 +21,11 @@
 
 
 def newton_kernel(
-    n_tm, n_unit, proj, w_hbm, bias_u, bias_c, start, guess_in, out,
-    w_all, w_diag, stage, mates, nears, own, packed, coefs, moves, relay_out, relay_in,
-    w_sem, mate_send, mate_recv, near_send, near_recv, coef_send, coef_recv, relay_send, relay_recv,
+    n_tm, n_unit, proj_hbm, w_hbm, bias_u_hbm, bias_c_hbm, start_hbm, guess_hbm, out,
+    proj, bias_u, bias_c, w_all, w_diag, stage, mates, nears, own, packed, coefs, moves, relay_out, relay_in,
+    in_sem, w_sem, mate_send, mate_recv, near_send, near_recv, coef_send, coef_recv, relay_send, relay_recv,
 ):
-    steps, width = guess_in.shape
+    steps, width = guess_hbm.shape
     blocks = width // BLOCK
     rows = steps * blocks
     group = min(GROUP, n_tm)
@@ -35,6 +35,18 @@
     place = lax.rem(time, group)
     reach = min(n_tm - 1, group if n_groups > 1 else group - 1)
 
+    smalls = [
+        pltpu.make_async_copy(source, target, in_sem.at[index])
+        for index, (source, target) in enumerate((
+            (guess_hbm, stage.at[0, pl.ds(0, steps)]),
+            (start_hbm, stage.at[0, pl.ds(steps, 1)]),
+            (proj_hbm, proj),
+            (bias_u_hbm, bias_u),
+            (bias_c_hbm, bias_c),
+        ))
+    ]
+    for load in smalls:
+        load.start()
     loads = [
         pltpu.make_async_copy(w_hbm.at[gate], w_all.at[gate], w_sem.at[gate]) for gate in range(3)
     ]
@@ -59,8 +71,8 @@
                         barrier, inc=1, device_id=to(there, lax.rem(unit + turn, n_unit)), device_id_type=MESH
                     )
 
-    stage[0, 0:steps, :] = guess_in[...]
-    stage[0, steps : steps + 1, :] = start[...]
+    for load in smalls[:2]:
+        load.wait()
     pl.semaphore_wait(barrier, greeted)
 
     def mate_copy(turn, away):
@@ -107,7 +119,7 @@
     def entering_from(held, away):
         return jnp.where(time == 0, held[steps : steps + 1, :], nears[(n_unit - away) % n_unit, steps - 1 : steps, :])
 
-    guess = guess_in[...]
+    guess = stage[0, 0:steps, :]
     previous = jnp.concatenate([entering_from(stage[0], 0), guess[: steps - 1]], axis=0)
     row = lax.broadcasted_iota(jnp.int32, (16, BLOCK), 0) % 8
 
@@ -119,6 +131,8 @@
 
         if turn == 0:
             for load in loads:
+                load.wait()
+            for load in smalls[2:]:
                 load.wait()
             for block in range(blocks):
                 first = pl.multiple_of(unit * width + block * BLOCK, BLOCK)
@@ -275,9 +289,12 @@
     result = pl.pallas_call(
         functools.partial(newton_kernel, n_tm, n_unit),
         out_shape=jax.ShapeDtypeStruct((steps, width), f32),
-        in_specs=[vmem, pl.BlockSpec(memory_space=pl.ANY), vmem, vmem, vmem, vmem],
+        in_specs=[pl.BlockSpec(memory_space=pltpu.HBM)] * 6,
         out_specs=vmem,
         scratch_shapes=[
+            pltpu.VMEM((3, steps, width), bf16),
+            pltpu.VMEM((1, width), f32),
+            pltpu.VMEM((1, width), f32),
             pltpu.VMEM((3, full, width), bf16),
             pltpu.VMEM((width, 3 * BLOCK), bf16),
             pltpu.VMEM((NEWTON, held, width), f32),
@@ -289,6 +306,7 @@
             pltpu.VMEM((rows + 8, BLOCK), f32),
             pltpu.VMEM((NEWTON, 8, BLOCK), f32),
             pltpu.VMEM((NEWTON, 8, BLOCK), f32),
+            dma((5,)),
             dma((3,)),
             dma((NEWTON, n_unit - 1)),
             dma((NEWTON, n_unit - 1)),
@@ -300,7 +318,7 @@
             dma((NEWTON,)),
         ],
         compiler_params=pltpu.CompilerParams(
-            collective_id=0, has_side_effects=True, vmem_limit_bytes=32 * 1024 * 1024
+            collective_id=0, has_side_effects=True, vmem_limit_bytes=60 * 1024 * 1024
         ),
         name="newton",
     )(

time: 30.6 us -> 26.3 us (0.86)
  local copies, waits for them, and re-layouts: 5.94 us -> 1.3 us
  Pallas kernels: 24.2 us -> 24.6 us
    unnamed x13 -> x1, local copies, waits for them, and re-layouts: 5.94 us -> 1.3 us
    pallas_call x1, Pallas kernels: 24.2 us -> 24.6 us  [shards(): pl.pallas_call(functools.partial(newton_kernel, n_tm, n_unit), out_shape=...]
where the time goes in v2:
time: 26.3 us; the launch traced here: 25.9 us
  Pallas kernels  24.6 us (94%)
  local copies, waits for them, and re-layouts  1.3 us (5%)
    pallas_call x1, Pallas kernels, shards(): pl.pallas_call(functools.partial(newton_kernel, n_tm, n_unit), out_shape=...  24.6 us
    unnamed x1, local copies, waits for them, and re-layouts  1.3 us

profile of v2, /device:TPU:31, one launch (start us, length us, event | category | flops | bytes accessed | tf_op | source)
XLA Modules:
  0.0 25.9 jit_solution(17585563727539474513)
XLA Ops:
  0.0 24.6 %newton.1 = f32[4,512]{1,0:T(4,128)} custom-call(bf16[3,4,512]{2,1,0:T(4,128)(2,1)} %bitcast.10, bf16[3,1024,512]{2,1,0:T(8,128)(2,1)} %bitcast.8, f32[1,512]{1,0:T(1,128)} %bitcast.12, f32[1,512]{1,0:T(1,128)} %bitcast.13, f32[1,512]{1,0:T(1,128)} %start_hbm.1, f32[4,512]{1,0:T(4,128)} %bitcast.11), custom_call_target="tpu_custom_call" | custom-call | tf_op jit(solution)/shard_map/newton/pallas_call | solution.py:289
  24.6 1.3 %copy.8 = f32[1,4,512]{2,1,0:T(4,128)} copy(f32[1,4,512]{2,1,0:T(4,128)} %bitcast.9) | data formatting | bytes 16384

commit v3 on v2

--- a/solution.py
+++ b/solution.py
@@ -1,4 +1,5 @@
 import functools
+import math
 
 import jax
 import jax.numpy as jnp
@@ -11,8 +12,6 @@
 NEWTON = 2
 GROUP = 8
 COEFS = 5
-FINE = (0, 4)
-SENT = COEFS + len(FINE)
 MESH = pl.DeviceIdType.MESH
 
 
@@ -22,17 +21,21 @@
 
 def newton_kernel(
     n_tm, n_unit, proj_hbm, w_hbm, bias_u_hbm, bias_c_hbm, start_hbm, guess_hbm, out,
-    proj, bias_u, bias_c, w_all, w_diag, stage, mates, nears, own, packed, coefs, moves, relay_out, relay_in,
-    in_sem, w_sem, mate_send, mate_recv, near_send, near_recv, coef_send, coef_recv, relay_send, relay_recv,
+    proj, bias_u, bias_c, w_all, w_diag, stage, mates, nears, own, coefs, found, moves, relay_out, relay_in,
+    in_sem, w_sem, mate_send, mate_recv, near_send, near_recv, coef_send, coef_recv, move_send, move_recv, relay_send, relay_recv,
 ):
     steps, width = guess_hbm.shape
     blocks = width // BLOCK
-    rows = steps * blocks
     group = min(GROUP, n_tm)
+    split = math.gcd(blocks, group)
+    count = blocks // split
+    rows = steps * count
     n_groups = n_tm // group
     time = lax.axis_index("tm")
     unit = lax.axis_index("unit")
     place = lax.rem(time, group)
+    column = lax.rem(place, split)
+    last_row = place >= group - split
     reach = min(n_tm - 1, group if n_groups > 1 else group - 1)
 
     smalls = [
@@ -91,16 +94,41 @@
 
     def coef_copy(turn, away):
         return pltpu.make_async_remote_copy(
-            src_ref=packed.at[turn], dst_ref=coefs.at[turn, away - 1],
-            send_sem=coef_send.at[turn, away - 1], recv_sem=coef_recv.at[turn, away - 1],
-            device_id=to(lax.rem(time + away, n_tm), unit), device_id_type=MESH,
+            src_ref=own.at[turn, lax.rem(place + away + group, split)], dst_ref=coefs.at[turn, place],
+            send_sem=coef_send.at[turn, away + split], recv_sem=coef_recv.at[turn, place],
+            device_id=to(lax.rem(time + away + n_tm, n_tm), unit), device_id_type=MESH,
+        )
+
+    def coef_wanted(away):
+        there = place + away
+        return (there < group) & (there >= place - column)
+
+    def coef_arrival(turn, source):
+        return pltpu.make_async_remote_copy(
+            src_ref=own.at[turn, 0], dst_ref=coefs.at[turn, source],
+            send_sem=coef_send.at[turn, 0], recv_sem=coef_recv.at[turn, source],
+            device_id=to(lax.rem(time + 1, n_tm), unit), device_id_type=MESH,
+        )
+
+    def move_copy(turn, member):
+        return pltpu.make_async_remote_copy(
+            src_ref=found.at[turn, member], dst_ref=moves.at[turn, column],
+            send_sem=move_send.at[turn, member], recv_sem=move_recv.at[turn, column],
+            device_id=to(time - column + member, unit), device_id_type=MESH,
+        )
+
+    def move_arrival(turn, member):
+        return pltpu.make_async_remote_copy(
+            src_ref=found.at[turn, member], dst_ref=moves.at[turn, member],
+            send_sem=move_send.at[turn, member], recv_sem=move_recv.at[turn, member],
+            device_id=to(time - column + member, unit), device_id_type=MESH,
         )
 
     def relay_copy(turn, target):
         return pltpu.make_async_remote_copy(
             src_ref=relay_out.at[turn], dst_ref=relay_in.at[turn],
             send_sem=relay_send.at[turn, target], recv_sem=relay_recv.at[turn],
-            device_id=to(lax.rem(time + 1 + target, n_tm), unit), device_id_type=MESH,
+            device_id=to(lax.rem(time - place + group + target * split + column, n_tm), unit), device_id_type=MESH,
         )
 
     for away in range(1, n_unit):
@@ -134,11 +162,12 @@
                 load.wait()
             for load in smalls[2:]:
                 load.wait()
-            for block in range(blocks):
-                first = pl.multiple_of(unit * width + block * BLOCK, BLOCK)
+            for block in range(count):
+                first = pl.multiple_of((column * count + block) * BLOCK, BLOCK)
+                inputs = pl.ds(pl.multiple_of(unit * width + first, BLOCK), BLOCK)
                 here = slice(block * BLOCK, (block + 1) * BLOCK)
                 for gate in range(3):
-                    w_diag[here, gate * BLOCK : (gate + 1) * BLOCK] = w_all[gate, pl.ds(first, BLOCK), here]
+                    w_diag[here, gate * BLOCK : (gate + 1) * BLOCK] = w_all[gate, inputs, pl.ds(first, BLOCK)]
 
         def product(panel, owner):
             first = pl.multiple_of(owner * width, width)
@@ -174,23 +203,21 @@
         )
         for index, value in enumerate(values):
             for block in range(blocks):
-                own[index, pl.ds(block, steps, stride=blocks), :] = value[:, block * BLOCK : (block + 1) * BLOCK]
-        packed[turn, 0:COEFS] = own[...].astype(jnp.bfloat16)
-        for slot, index in enumerate(FINE):
-            full = own[index]
-            packed[turn, COEFS + slot] = (full - full.astype(jnp.bfloat16).astype(jnp.float32)).astype(jnp.bfloat16)
-
-        for away in range(group - 1, 0, -1):
-            @pl.when(place + away < group)
+                first = index * rows + block % count
+                where = pl.ds(first, steps, stride=count) if count > 1 else pl.ds(first, steps)
+                own[turn, block // count, where, :] = value[:, block * BLOCK : (block + 1) * BLOCK]
+        for away in list(range(group - 1, 0, -1)) + list(range(-1, -split, -1)):
+            @pl.when(coef_wanted(away))
             def _():
                 coef_copy(turn, away).start()
+        coefs[turn, place] = own[turn, column]
 
         def step(delta, five):
             high = delta.astype(jnp.bfloat16).astype(jnp.float32)
             both = jnp.concatenate([high, delta - high], axis=0)
-            left = jnp.concatenate(
-                [jnp.where(row == block, both, 0.0) for block in range(blocks)], axis=1
-            ).astype(jnp.bfloat16)
+            if count > 1:
+                both = jnp.concatenate([jnp.where(row == block, both, 0.0) for block in range(count)], axis=1)
+            left = both.astype(jnp.bfloat16)
             terms = jnp.dot(left, w_diag[...], preferred_element_type=jnp.float32)
             terms = terms[:8] + terms[8:]
             fresh, a, c, d, gap = five
@@ -199,26 +226,18 @@
                 + c * terms[:, BLOCK : 2 * BLOCK] + d * terms[:, 2 * BLOCK :]
             )
 
-        def at_step(table, t):
-            def pick(value):
-                part = value[t * blocks : (t + 1) * blocks]
-                return jnp.concatenate([part] * (8 // blocks), axis=0)
-
-            return [pick(table[index]) for index in range(COEFS)]
+        def at_step(source, t):
+            def pick(index):
+                first = index * rows + t * count
+                part = coefs[turn, source, first : first + count, :]
+                return jnp.concatenate([part] * (8 // count), axis=0) if count > 1 else jnp.broadcast_to(part, (8, BLOCK))
+
+            return [pick(index) for index in range(COEFS)]
 
         def pass_block(source, delta):
-            away = place - source
-            slot = away - 1
-            pltpu.make_async_remote_copy(
-                src_ref=packed.at[turn], dst_ref=coefs.at[turn, slot],
-                send_sem=coef_send.at[turn, slot], recv_sem=coef_recv.at[turn, slot],
-                device_id=to(lax.rem(time + 1, n_tm), unit), device_id_type=MESH,
-            ).wait_recv()
-            table = [coefs[turn, slot, index].astype(jnp.float32) for index in range(SENT)]
-            for low, index in enumerate(FINE):
-                table[index] = table[index] + table[COEFS + low]
+            coef_arrival(turn, source).wait_recv()
             for t in range(steps):
-                delta = step(delta, at_step(table, t))
+                delta = step(delta, at_step(source, t))
             return delta
 
         delta = jnp.zeros((8, BLOCK), jnp.float32)
@@ -234,24 +253,44 @@
                 relay_copy(turn, 0).wait_recv()
 
             delta = relay_in_now[...]
-        delta = lax.fori_loop(0, place, pass_block, delta)
-        moves[0:blocks, :] = delta[:blocks]
-        table = own[...]
-        for t in range(steps):
-            delta = step(delta, at_step(table, t))
-            moves[(t + 1) * blocks : (t + 2) * blocks, :] = delta[:blocks]
+        delta = lax.fori_loop(0, place - column, pass_block, delta)
+        for member in range(split):
+            source = place - column + member
+
+            @pl.when(column != member)
+            def _():
+                coef_arrival(turn, source).wait_recv()
+
+            found[turn, member, 0:count, :] = delta[:count]
+            for t in range(steps):
+                delta = step(delta, at_step(source, t))
+                found[turn, member, (t + 1) * count : (t + 2) * count, :] = delta[:count]
+
+            @pl.when(column != member)
+            def _():
+                move_copy(turn, member).start()
+
+        moves[turn, column] = found[turn, column]
         if n_groups > 1:
             relay_out[turn] = delta
 
-            @pl.when((place == group - 1) & (time < n_tm - 1))
-            def _():
-                for target in range(group):
+            @pl.when(last_row & (time < n_tm - split))
+            def _():
+                for target in range(group // split):
                     relay_copy(turn, target).start()
 
+        for member in range(split):
+            @pl.when(column != member)
+            def _():
+                move_arrival(turn, member).wait_recv()
+
         def moved(skip):
-            return jnp.concatenate(
-                [moves[pl.ds(skip * blocks + block, steps, stride=blocks), :] for block in range(blocks)], axis=1
-            )
+            parts = []
+            for block in range(blocks):
+                first = skip * count + block % count
+                where = pl.ds(first, steps, stride=count) if count > 1 else pl.ds(first, steps)
+                parts.append(moves[turn, block // count, where, :])
+            return jnp.concatenate(parts, axis=1)
 
         guess = guess + moved(1)
         if turn < NEWTON - 1:
@@ -266,22 +305,31 @@
     for turn in range(NEWTON):
         for away in range(1, n_unit):
             mate_copy(turn, away).wait_send()
-        for away in range(1, group):
-            @pl.when(place + away < group)
-            def _():
-                coef_copy(turn, away).wait_send()
+        for away in range(1 - split, group):
+            if away:
+                @pl.when(coef_wanted(away))
+                def _():
+                    coef_copy(turn, away).wait_send()
+        for member in range(split):
+            @pl.when(column != member)
+            def _():
+                move_copy(turn, member).wait_send()
         if n_groups > 1:
-            @pl.when((place == group - 1) & (time < n_tm - 1))
-            def _():
-                for target in range(group):
+            @pl.when(last_row & (time < n_tm - split))
+            def _():
+                for target in range(group // split):
                     relay_copy(turn, target).wait_send()
 
 
 def shards(n_tm, n_unit, projections, recurrent, update_bias, candidate_bias, start_state, initial_guess):
     _, steps, _, width = projections.shape
     full = recurrent.shape[0]
-    rows = steps * (width // BLOCK)
+    blocks = width // BLOCK
     group = min(GROUP, n_tm)
+    split = math.gcd(blocks, group)
+    count = blocks // split
+    sent = 8 * pl.cdiv(COEFS * steps * count, 8)
+    kept = 8 * pl.cdiv((steps + 1) * count, 8)
     vmem = pl.BlockSpec(memory_space=pltpu.VMEM)
     f32, bf16 = jnp.float32, jnp.bfloat16
     held = 8 * pl.cdiv(steps + 1, 8)
@@ -296,14 +344,14 @@
             pltpu.VMEM((1, width), f32),
             pltpu.VMEM((1, width), f32),
             pltpu.VMEM((3, full, width), bf16),
-            pltpu.VMEM((width, 3 * BLOCK), bf16),
+            pltpu.VMEM((count * BLOCK, 3 * BLOCK), bf16),
             pltpu.VMEM((NEWTON, held, width), f32),
             pltpu.VMEM((NEWTON, n_unit - 1, held, width), f32),
             pltpu.VMEM((n_unit, held, width), f32),
-            pltpu.VMEM((COEFS, rows, BLOCK), f32),
-            pltpu.VMEM((NEWTON, SENT, rows, BLOCK), bf16),
-            pltpu.VMEM((NEWTON, group - 1, SENT, rows, BLOCK), bf16),
-            pltpu.VMEM((rows + 8, BLOCK), f32),
+            pltpu.VMEM((NEWTON, split, sent, BLOCK), f32),
+            pltpu.VMEM((NEWTON, group, sent, BLOCK), f32),
+            pltpu.VMEM((NEWTON, split, kept, BLOCK), f32),
+            pltpu.VMEM((NEWTON, split, kept, BLOCK), f32),
             pltpu.VMEM((NEWTON, 8, BLOCK), f32),
             pltpu.VMEM((NEWTON, 8, BLOCK), f32),
             dma((5,)),
@@ -312,9 +360,11 @@
             dma((NEWTON, n_unit - 1)),
             dma((n_unit,)),
             dma((n_unit,)),
-            dma((NEWTON, group - 1)),
-            dma((NEWTON, group - 1)),
+            dma((NEWTON, group + split)),
             dma((NEWTON, group)),
+            dma((NEWTON, split)),
+            dma((NEWTON, split)),
+            dma((NEWTON, group // split)),
             dma((NEWTON,)),
         ],
         compiler_params=pltpu.CompilerParams(

time: 26.3 us -> 28.2 us (1.072)
  the two profiles are of different devices: /device:TPU:31 before, /device:TPU:26 now
where the time goes in v3:
time: 28.2 us; the launch traced here: 27.9 us
  Pallas kernels  26.6 us (94%)
  local copies, waits for them, and re-layouts  1.3 us (5%)
    pallas_call x1, Pallas kernels, shards(): pl.pallas_call(functools.partial(newton_kernel, n_tm, n_unit), out_shape=...  26.6 us
    unnamed x1, local copies, waits for them, and re-layouts  1.3 us

profile of v3, /device:TPU:26, one launch (start us, length us, event | category | flops | bytes accessed | tf_op | source)
XLA Modules:
  0.0 27.9 jit_solution(3140104937997446406)
XLA Ops:
  0.0 26.6 %newton.1 = f32[4,512]{1,0:T(4,128)} custom-call(bf16[3,4,512]{2,1,0:T(4,128)(2,1)} %bitcast.10, bf16[3,1024,512]{2,1,0:T(8,128)(2,1)} %bitcast.8, f32[1,512]{1,0:T(1,128)} %bitcast.12, f32[1,512]{1,0:T(1,128)} %bitcast.13, f32[1,512]{1,0:T(1,128)} %start_hbm.1, f32[4,512]{1,0:T(4,128)} %bitcast.11), custom_call_target="tpu_custom_call" | custom-call | tf_op jit(solution)/shard_map/newton/pallas_call | solution.py:337
  26.6 1.3 %copy.8 = f32[1,4,512]{2,1,0:T(4,128)} copy(f32[1,4,512]{2,1,0:T(4,128)} %bitcast.9) | data formatting | bytes 16384

commit v4 on v2

--- a/solution.py
+++ b/solution.py
@@ -28,6 +28,7 @@
     steps, width = guess_hbm.shape
     blocks = width // BLOCK
     rows = steps * blocks
+    side = 2 if blocks % 2 == 0 else 1
     group = min(GROUP, n_tm)
     n_groups = n_tm // group
     time = lax.axis_index("tm")
@@ -121,7 +122,12 @@
 
     guess = stage[0, 0:steps, :]
     previous = jnp.concatenate([entering_from(stage[0], 0), guess[: steps - 1]], axis=0)
-    row = lax.broadcasted_iota(jnp.int32, (16, BLOCK), 0) % 8
+    row = lax.broadcasted_iota(jnp.int32, (8, BLOCK), 0)
+
+    def gate_column(pair, gate):
+        pairs = blocks // side
+        return (2 * pair + gate if gate < 2 else 2 * pairs + pair) * BLOCK
+
 
     for turn in range(NEWTON):
         if turn:
@@ -137,8 +143,10 @@
             for block in range(blocks):
                 first = pl.multiple_of(unit * width + block * BLOCK, BLOCK)
                 here = slice(block * BLOCK, (block + 1) * BLOCK)
+                depth = block % side * BLOCK
                 for gate in range(3):
-                    w_diag[here, gate * BLOCK : (gate + 1) * BLOCK] = w_all[gate, pl.ds(first, BLOCK), here]
+                    column = gate_column(block // side, gate)
+                    w_diag[depth : depth + BLOCK, column : column + BLOCK] = w_all[gate, pl.ds(first, BLOCK), here]
 
         def product(panel, owner):
             first = pl.multiple_of(owner * width, width)
@@ -148,55 +156,23 @@
                 for gate in range(3)
             ]
 
-        rec = product(previous, unit)
-        for away in range(1, n_unit):
-            mate_copy(turn, away).wait_recv()
-            held = mates[turn, away - 1]
-            if turn:
-                panel = held[:steps]
-            else:
-                panel = jnp.concatenate([entering_from(held, n_unit - away), held[: steps - 1]], axis=0)
-            rec = [x + y for x, y in zip(rec, product(panel, lax.rem(unit + n_unit - away, n_unit)))]
-
-        update_in = proj[0].astype(jnp.float32) + rec[0] + bias_u[...]
-        update = jax.nn.sigmoid(update_in)
-        fresh = jax.nn.sigmoid(-update_in)
-        reset = jax.nn.sigmoid(proj[1].astype(jnp.float32) + rec[1])
-        cand_rec = rec[2] + bias_c[...]
-        cand = jnp.tanh(proj[2].astype(jnp.float32) + reset * cand_rec)
-        coef_d = fresh * (1.0 - cand * cand) * reset
-        values = (
-            fresh,
-            (previous - cand) * update * fresh,
-            coef_d * cand_rec * (1.0 - reset),
-            coef_d,
-            fresh * cand + update * previous - guess,
-        )
-        for index, value in enumerate(values):
-            for block in range(blocks):
-                own[index, pl.ds(block, steps, stride=blocks), :] = value[:, block * BLOCK : (block + 1) * BLOCK]
-        packed[turn, 0:COEFS] = own[...].astype(jnp.bfloat16)
-        for slot, index in enumerate(FINE):
-            full = own[index]
-            packed[turn, COEFS + slot] = (full - full.astype(jnp.bfloat16).astype(jnp.float32)).astype(jnp.bfloat16)
-
-        for away in range(group - 1, 0, -1):
-            @pl.when(place + away < group)
-            def _():
-                coef_copy(turn, away).start()
-
         def step(delta, five):
-            high = delta.astype(jnp.bfloat16).astype(jnp.float32)
-            both = jnp.concatenate([high, delta - high], axis=0)
             left = jnp.concatenate(
-                [jnp.where(row == block, both, 0.0) for block in range(blocks)], axis=1
+                [jnp.where((row % side == depth) & (row < blocks), delta, 0.0) for depth in range(side)], axis=1
             ).astype(jnp.bfloat16)
             terms = jnp.dot(left, w_diag[...], preferred_element_type=jnp.float32)
-            terms = terms[:8] + terms[8:]
+
+            def of_gate(gate):
+                value = None
+                for pair in range(blocks // side):
+                    column = gate_column(pair, gate)
+                    part = terms[:, column : column + BLOCK]
+                    value = part if value is None else jnp.where(row // side == pair, part, value)
+                return value
+
             fresh, a, c, d, gap = five
             return (
-                (gap + delta - fresh * delta) + a * terms[:, :BLOCK]
-                + c * terms[:, BLOCK : 2 * BLOCK] + d * terms[:, 2 * BLOCK :]
+                (gap + delta - fresh * delta) + a * of_gate(0) + c * of_gate(1) + d * of_gate(2)
             )
 
         def at_step(table, t):
@@ -221,7 +197,49 @@
                 delta = step(delta, at_step(table, t))
             return delta
 
-        delta = jnp.zeros((8, BLOCK), jnp.float32)
+        rec = product(previous, unit)
+        early = jnp.int32(0)
+        if turn == 0 or n_groups > 1:
+            delta = jnp.zeros((8, BLOCK), jnp.float32)
+        else:
+            early = (2 * place) // group
+            delta = lax.fori_loop(0, early, pass_block, jnp.zeros((8, BLOCK), jnp.float32))
+        for away in range(1, n_unit):
+            mate_copy(turn, away).wait_recv()
+            held = mates[turn, away - 1]
+            if turn:
+                panel = held[:steps]
+            else:
+                panel = jnp.concatenate([entering_from(held, n_unit - away), held[: steps - 1]], axis=0)
+            rec = [x + y for x, y in zip(rec, product(panel, lax.rem(unit + n_unit - away, n_unit)))]
+
+        update_in = proj[0].astype(jnp.float32) + rec[0] + bias_u[...]
+        update = jax.nn.sigmoid(update_in)
+        fresh = jax.nn.sigmoid(-update_in)
+        reset = jax.nn.sigmoid(proj[1].astype(jnp.float32) + rec[1])
+        cand_rec = rec[2] + bias_c[...]
+        cand = jnp.tanh(proj[2].astype(jnp.float32) + reset * cand_rec)
+        coef_d = fresh * (1.0 - cand * cand) * reset
+        values = (
+            fresh,
+            (previous - cand) * update * fresh,
+            coef_d * cand_rec * (1.0 - reset),
+            coef_d,
+            fresh * cand + update * previous - guess,
+        )
+        for index, value in enumerate(values):
+            for block in range(blocks):
+                own[index, pl.ds(block, steps, stride=blocks), :] = value[:, block * BLOCK : (block + 1) * BLOCK]
+        packed[turn, 0:COEFS] = own[...].astype(jnp.bfloat16)
+        for slot, index in enumerate(FINE):
+            full = own[index]
+            packed[turn, COEFS + slot] = (full - full.astype(jnp.bfloat16).astype(jnp.float32)).astype(jnp.bfloat16)
+
+        for away in range(group - 1, 0, -1):
+            @pl.when(place + away < group)
+            def _():
+                coef_copy(turn, away).start()
+
         if n_groups > 1:
             relay_in_now = relay_in.at[turn]
 
@@ -234,7 +252,7 @@
                 relay_copy(turn, 0).wait_recv()
 
             delta = relay_in_now[...]
-        delta = lax.fori_loop(0, place, pass_block, delta)
+        delta = lax.fori_loop(early, place, pass_block, delta)
         moves[0:blocks, :] = delta[:blocks]
         table = own[...]
         for t in range(steps):
@@ -282,6 +300,7 @@
     full = recurrent.shape[0]
     rows = steps * (width // BLOCK)
     group = min(GROUP, n_tm)
+    side = 2 if width // BLOCK % 2 == 0 else 1
     vmem = pl.BlockSpec(memory_space=pltpu.VMEM)
     f32, bf16 = jnp.float32, jnp.bfloat16
     held = 8 * pl.cdiv(steps + 1, 8)
@@ -296,7 +315,7 @@
             pltpu.VMEM((1, width), f32),
             pltpu.VMEM((1, width), f32),
             pltpu.VMEM((3, full, width), bf16),
-            pltpu.VMEM((width, 3 * BLOCK), bf16),
+            pltpu.VMEM((side * BLOCK, 3 * (width // side)), bf16),
             pltpu.VMEM((NEWTON, held, width), f32),
             pltpu.VMEM((NEWTON, n_unit - 1, held, width), f32),
             pltpu.VMEM((n_unit, held, width), f32),

time: 26.3 us -> 26.4 us (level)
  the two profiles are of different devices: /device:TPU:31 before, /device:TPU:26 now
where the time goes in v4:
time: 26.4 us; the launch traced here: 26.1 us
  Pallas kernels  24.8 us (94%)
  local copies, waits for them, and re-layouts  1.3 us (5%)
    pallas_call x1, Pallas kernels, shards(): pl.pallas_call(functools.partial(newton_kernel, n_tm, n_unit), out_shape=...  24.8 us
    unnamed x1, local copies, waits for them, and re-layouts  1.3 us

profile of v4, /device:TPU:26, one launch (start us, length us, event | category | flops | bytes accessed | tf_op | source)
XLA Modules:
  0.0 26.1 jit_solution(1200486075554647181)
XLA Ops:
  0.0 24.8 %newton.1 = f32[4,512]{1,0:T(4,128)} custom-call(bf16[3,4,512]{2,1,0:T(4,128)(2,1)} %bitcast.10, bf16[3,1024,512]{2,1,0:T(8,128)(2,1)} %bitcast.8, f32[1,512]{1,0:T(1,128)} %bitcast.12, f32[1,512]{1,0:T(1,128)} %bitcast.13, f32[1,512]{1,0:T(1,128)} %start_hbm.1, f32[4,512]{1,0:T(4,128)} %bitcast.11), custom_call_target="tpu_custom_call" | custom-call | tf_op jit(solution)/shard_map/newton/pallas_call | solution.py:308
  24.8 1.3 %copy.8 = f32[1,4,512]{2,1,0:T(4,128)} copy(f32[1,4,512]{2,1,0:T(4,128)} %bitcast.9) | data formatting | bytes 16384

commit v5 on v4

--- a/solution.py
+++ b/solution.py
@@ -23,7 +23,7 @@
 def newton_kernel(
     n_tm, n_unit, proj_hbm, w_hbm, bias_u_hbm, bias_c_hbm, start_hbm, guess_hbm, out,
     proj, bias_u, bias_c, w_all, w_diag, stage, mates, nears, own, packed, coefs, moves, relay_out, relay_in,
-    in_sem, w_sem, mate_send, mate_recv, near_send, near_recv, coef_send, coef_recv, relay_send, relay_recv,
+    in_sem, w_sem, mate_send, mate_recv, near_send, near_recv, coef_send, coef_recv, pass_send, relay_send, relay_recv,
 ):
     steps, width = guess_hbm.shape
     blocks = width // BLOCK
@@ -34,6 +34,9 @@
     time = lax.axis_index("tm")
     unit = lax.axis_index("unit")
     place = lax.rem(time, group)
+    side_of = lax.rem(place, 2)
+    pair_row = lax.div(place, 2)
+    straight = [away for away in range(group - 1, 0, -1) if away == 1 or away % 2 == 0]
     reach = min(n_tm - 1, group if n_groups > 1 else group - 1)
 
     smalls = [
@@ -97,6 +100,13 @@
             device_id=to(lax.rem(time + away, n_tm), unit), device_id_type=MESH,
         )
 
+    def pass_on(turn, distance):
+        return pltpu.make_async_remote_copy(
+            src_ref=coefs.at[turn, distance - 1], dst_ref=coefs.at[turn, distance - 2 * side_of],
+            send_sem=pass_send.at[turn, lax.div(distance, 2) - 1], recv_sem=coef_recv.at[turn, distance - 2 * side_of],
+            device_id=to(time + 1 - 2 * side_of, unit), device_id_type=MESH,
+        )
+
     def relay_copy(turn, target):
         return pltpu.make_async_remote_copy(
             src_ref=relay_out.at[turn], dst_ref=relay_in.at[turn],
@@ -182,14 +192,22 @@
 
             return [pick(table[index]) for index in range(COEFS)]
 
-        def pass_block(source, delta):
-            away = place - source
-            slot = away - 1
+        def arrival(slot):
             pltpu.make_async_remote_copy(
                 src_ref=packed.at[turn], dst_ref=coefs.at[turn, slot],
                 send_sem=coef_send.at[turn, slot], recv_sem=coef_recv.at[turn, slot],
                 device_id=to(lax.rem(time + 1, n_tm), unit), device_id_type=MESH,
             ).wait_recv()
+
+        def take(pair):
+            distance = 2 * (pair_row - pair)
+            arrival(distance - 1)
+
+            @pl.when((side_of == 0) | (distance >= 4))
+            def _():
+                pass_on(turn, distance).start()
+
+        def pass_block(slot, delta):
             table = [coefs[turn, slot, index].astype(jnp.float32) for index in range(SENT)]
             for low, index in enumerate(FINE):
                 table[index] = table[index] + table[COEFS + low]
@@ -197,13 +215,30 @@
                 delta = step(delta, at_step(table, t))
             return delta
 
+        def pass_pair(pair, delta):
+            @pl.when(pair + 1 < pair_row)
+            def _():
+                take(pair + 1)
+
+            slot = place - 2 * pair - 1
+
+            @pl.when(side_of == 1)
+            def _():
+                arrival(slot)
+
+            delta = pass_block(slot, delta)
+
+            @pl.when(side_of == 0)
+            def _():
+                arrival(slot - 1)
+
+            return pass_block(slot - 1, delta)
+
+        def pass_last(_, delta):
+            arrival(0)
+            return pass_block(0, delta)
+
         rec = product(previous, unit)
-        early = jnp.int32(0)
-        if turn == 0 or n_groups > 1:
-            delta = jnp.zeros((8, BLOCK), jnp.float32)
-        else:
-            early = (2 * place) // group
-            delta = lax.fori_loop(0, early, pass_block, jnp.zeros((8, BLOCK), jnp.float32))
         for away in range(1, n_unit):
             mate_copy(turn, away).wait_recv()
             held = mates[turn, away - 1]
@@ -235,11 +270,16 @@
             full = own[index]
             packed[turn, COEFS + slot] = (full - full.astype(jnp.bfloat16).astype(jnp.float32)).astype(jnp.bfloat16)
 
-        for away in range(group - 1, 0, -1):
+        for away in straight:
             @pl.when(place + away < group)
             def _():
                 coef_copy(turn, away).start()
 
+        @pl.when(pair_row > 0)
+        def _():
+            take(0)
+
+        delta = jnp.zeros((8, BLOCK), jnp.float32)
         if n_groups > 1:
             relay_in_now = relay_in.at[turn]
 
@@ -252,7 +292,8 @@
                 relay_copy(turn, 0).wait_recv()
 
             delta = relay_in_now[...]
-        delta = lax.fori_loop(early, place, pass_block, delta)
+        delta = lax.fori_loop(0, pair_row, pass_pair, delta)
+        delta = lax.fori_loop(0, side_of, pass_last, delta)
         moves[0:blocks, :] = delta[:blocks]
         table = own[...]
         for t in range(steps):
@@ -284,10 +325,14 @@
     for turn in range(NEWTON):
         for away in range(1, n_unit):
             mate_copy(turn, away).wait_send()
-        for away in range(1, group):
+        for away in straight:
             @pl.when(place + away < group)
             def _():
                 coef_copy(turn, away).wait_send()
+        for distance in range(2, group, 2):
+            @pl.when((place >= distance) & ((side_of == 0) | (distance >= 4)))
+            def _():
+                pass_on(turn, distance).wait_send()
         if n_groups > 1:
             @pl.when((place == group - 1) & (time < n_tm - 1))
             def _():
@@ -333,6 +378,7 @@
             dma((n_unit,)),
             dma((NEWTON, group - 1)),
             dma((NEWTON, group - 1)),
+            dma((NEWTON, group // 2)),
             dma((NEWTON, group)),
             dma((NEWTON,)),
         ],

time: 26.4 us -> 31.6 us (1.20)
  the two profiles are of different devices: /device:TPU:26 before, /device:TPU:31 now
where the time goes in v5:
time: 31.6 us; the launch traced here: 31.3 us
  Pallas kernels  30 us (95%)
  local copies, waits for them, and re-layouts  1.3 us (4%)
    pallas_call x1, Pallas kernels, shards(): pl.pallas_call(functools.partial(newton_kernel, n_tm, n_unit), out_shape=...  30 us
    unnamed x1, local copies, waits for them, and re-layouts  1.3 us

profile of v5, /device:TPU:31, one launch (start us, length us, event | category | flops | bytes accessed | tf_op | source)
XLA Modules:
  0.0 31.3 jit_solution(15730797731805410077)
XLA Ops:
  0.0 30.0 %newton.1 = f32[4,512]{1,0:T(4,128)} custom-call(bf16[3,4,512]{2,1,0:T(4,128)(2,1)} %bitcast.10, bf16[3,1024,512]{2,1,0:T(8,128)(2,1)} %bitcast.8, f32[1,512]{1,0:T(1,128)} %bitcast.12, f32[1,512]{1,0:T(1,128)} %bitcast.13, f32[1,512]{1,0:T(1,128)} %start_hbm.1, f32[4,512]{1,0:T(4,128)} %bitcast.11), custom_call_target="tpu_custom_call" | custom-call | tf_op jit(solution)/shard_map/newton/pallas_call | solution.py:353
  30.0 1.3 %copy.8 = f32[1,4,512]{2,1,0:T(4,128)} copy(f32[1,4,512]{2,1,0:T(4,128)} %bitcast.9) | data formatting | bytes 16384

commit v6 on v4

--- a/solution.py
+++ b/solution.py
@@ -9,7 +9,7 @@
 
 BLOCK = 128
 NEWTON = 2
-GROUP = 8
+GROUP = 2
 COEFS = 5
 FINE = (0, 4)
 SENT = COEFS + len(FINE)

time: 26.4 us -> 23.9 us (0.905)
  the two profiles are of different devices: /device:TPU:26 before, /device:TPU:31 now
where the time goes in v6:
time: 23.9 us; the launch traced here: 23.6 us
  Pallas kernels  22.3 us (93%)
  local copies, waits for them, and re-layouts  1.3 us (5%)
    pallas_call x1, Pallas kernels, shards(): pl.pallas_call(functools.partial(newton_kernel, n_tm, n_unit), out_shape=...  22.3 us
    unnamed x1, local copies, waits for them, and re-layouts  1.3 us

profile of v6, /device:TPU:31, one launch (start us, length us, event | category | flops | bytes accessed | tf_op | source)
XLA Modules:
  0.0 23.6 jit_solution(1656015607898927474)
XLA Ops:
  0.0 22.3 %newton.1 = f32[4,512]{1,0:T(4,128)} custom-call(bf16[3,4,512]{2,1,0:T(4,128)(2,1)} %bitcast.10, bf16[3,1024,512]{2,1,0:T(8,128)(2,1)} %bitcast.8, f32[1,512]{1,0:T(1,128)} %bitcast.12, f32[1,512]{1,0:T(1,128)} %bitcast.13, f32[1,512]{1,0:T(1,128)} %start_hbm.1, f32[4,512]{1,0:T(4,128)} %bitcast.11), custom_call_target="tpu_custom_call" | custom-call | tf_op jit(solution)/shard_map/newton/pallas_call | solution.py:308
  22.3 1.3 %copy.8 = f32[1,4,512]{2,1,0:T(4,128)} copy(f32[1,4,512]{2,1,0:T(4,128)} %bitcast.9) | data formatting | bytes 16384

commit v7 on v6

--- a/solution.py
+++ b/solution.py
@@ -9,7 +9,7 @@
 
 BLOCK = 128
 NEWTON = 2
-GROUP = 2
+GROUP = 4
 COEFS = 5
 FINE = (0, 4)
 SENT = COEFS + len(FINE)
@@ -112,6 +112,23 @@
         for away in range(n_unit):
             near_copy(away).start()
 
+    def gate_column(pair, gate):
+        pairs = blocks // side
+        return (2 * pair + gate if gate < 2 else 2 * pairs + pair) * BLOCK
+
+
+    for load in loads:
+        load.wait()
+    for load in smalls[2:]:
+        load.wait()
+    for block in range(blocks):
+        first = pl.multiple_of(unit * width + block * BLOCK, BLOCK)
+        here = slice(block * BLOCK, (block + 1) * BLOCK)
+        depth = block % side * BLOCK
+        for gate in range(3):
+            column = gate_column(block // side, gate)
+            w_diag[depth : depth + BLOCK, column : column + BLOCK] = w_all[gate, pl.ds(first, BLOCK), here]
+
     @pl.when(time > 0)
     def _():
         for away in range(n_unit):
@@ -123,30 +140,12 @@
     guess = stage[0, 0:steps, :]
     previous = jnp.concatenate([entering_from(stage[0], 0), guess[: steps - 1]], axis=0)
     row = lax.broadcasted_iota(jnp.int32, (8, BLOCK), 0)
-
-    def gate_column(pair, gate):
-        pairs = blocks // side
-        return (2 * pair + gate if gate < 2 else 2 * pairs + pair) * BLOCK
-
 
     for turn in range(NEWTON):
         if turn:
             stage[turn, 0:steps, :] = previous
             for away in range(1, n_unit):
                 mate_copy(turn, away).start()
-
-        if turn == 0:
-            for load in loads:
-                load.wait()
-            for load in smalls[2:]:
-                load.wait()
-            for block in range(blocks):
-                first = pl.multiple_of(unit * width + block * BLOCK, BLOCK)
-                here = slice(block * BLOCK, (block + 1) * BLOCK)
-                depth = block % side * BLOCK
-                for gate in range(3):
-                    column = gate_column(block // side, gate)
-                    w_diag[depth : depth + BLOCK, column : column + BLOCK] = w_all[gate, pl.ds(first, BLOCK), here]
 
         def product(panel, owner):
             first = pl.multiple_of(owner * width, width)
@@ -263,7 +262,7 @@
 
             @pl.when((place == group - 1) & (time < n_tm - 1))
             def _():
-                for target in range(group):
+                for target in reversed(range(group)):
                     relay_copy(turn, target).start()
 
         def moved(skip):

time: 23.9 us -> 22.5 us (0.941)
  Pallas kernels: 22.3 us -> 20.7 us
    pallas_call x1, Pallas kernels: 22.3 us -> 20.7 us  [shards(): pl.pallas_call(functools.partial(newton_kernel, n_tm, n_unit), out_shape=...]
where the time goes in v7:
time: 22.5 us; the launch traced here: 22.1 us
  Pallas kernels  20.7 us (92%)
  local copies, waits for them, and re-layouts  1.3 us (6%)
    pallas_call x1, Pallas kernels, shards(): pl.pallas_call(functools.partial(newton_kernel, n_tm, n_unit), out_shape=...  20.7 us
    unnamed x1, local copies, waits for them, and re-layouts  1.3 us

profile of v7, /device:TPU:31, one launch (start us, length us, event | category | flops | bytes accessed | tf_op | source)
XLA Modules:
  0.0 22.1 jit_solution(7232985623401825913)
XLA Ops:
  0.0 20.7 %newton.1 = f32[4,512]{1,0:T(4,128)} custom-call(bf16[3,4,512]{2,1,0:T(4,128)(2,1)} %bitcast.10, bf16[3,1024,512]{2,1,0:T(8,128)(2,1)} %bitcast.8, f32[1,512]{1,0:T(1,128)} %bitcast.12, f32[1,512]{1,0:T(1,128)} %bitcast.13, f32[1,512]{1,0:T(1,128)} %start_hbm.1, f32[4,512]{1,0:T(4,128)} %bitcast.11), custom_call_target="tpu_custom_call" | custom-call | tf_op jit(solution)/shard_map/newton/pallas_call | solution.py:307
  20.8 1.3 %copy.8 = f32[1,4,512]{2,1,0:T(4,128)} copy(f32[1,4,512]{2,1,0:T(4,128)} %bitcast.9) | data formatting | bytes 16384

commit v8 on v7

--- a/solution.py
+++ b/solution.py
@@ -22,7 +22,7 @@
 
 def newton_kernel(
     n_tm, n_unit, proj_hbm, w_hbm, bias_u_hbm, bias_c_hbm, start_hbm, guess_hbm, out,
-    proj, bias_u, bias_c, w_all, w_diag, stage, mates, nears, own, packed, coefs, moves, relay_out, relay_in,
+    proj, bias_u, bias_c, w_all, w_diag, stage, mates, nears, own, packed, coefs, ready, moves, relay_out, relay_in,
     in_sem, w_sem, mate_send, mate_recv, near_send, near_recv, coef_send, coef_recv, relay_send, relay_recv,
 ):
     steps, width = guess_hbm.shape
@@ -54,6 +54,7 @@
     for load in loads:
         load.start()
 
+    ready[...] = jnp.zeros(ready.shape, jnp.float32)
     barrier = pltpu.get_barrier_semaphore()
     greeted = jnp.int32(n_unit - 1)
     for away in range(1, n_unit):
@@ -174,16 +175,13 @@
                 (gap + delta - fresh * delta) + a * of_gate(0) + c * of_gate(1) + d * of_gate(2)
             )
 
-        def at_step(table, t):
-            def pick(value):
-                part = value[t * blocks : (t + 1) * blocks]
-                return jnp.concatenate([part] * (8 // blocks), axis=0)
-
-            return [pick(table[index]) for index in range(COEFS)]
-
-        def pass_block(source, delta):
-            away = place - source
-            slot = away - 1
+        def spread(slot, table):
+            for index in range(COEFS):
+                for t in range(steps):
+                    ready[slot, index, t, 0:blocks, :] = table[index][t * blocks : (t + 1) * blocks]
+
+        def prepare(source):
+            slot = place - source - 1
             pltpu.make_async_remote_copy(
                 src_ref=packed.at[turn], dst_ref=coefs.at[turn, slot],
                 send_sem=coef_send.at[turn, slot], recv_sem=coef_recv.at[turn, slot],
@@ -192,17 +190,25 @@
             table = [coefs[turn, slot, index].astype(jnp.float32) for index in range(SENT)]
             for low, index in enumerate(FINE):
                 table[index] = table[index] + table[COEFS + low]
+            spread(slot, table)
+
+        def prepare_ahead(source, carry):
+            prepare(source)
+            return carry
+
+        def at_step(slot, t):
+            return [ready[slot, index, t] for index in range(COEFS)]
+
+        def pass_block(source, delta):
+            @pl.when(source >= ahead)
+            def _():
+                prepare(source)
+
             for t in range(steps):
-                delta = step(delta, at_step(table, t))
+                delta = step(delta, at_step(place - source - 1, t))
             return delta
 
         rec = product(previous, unit)
-        early = jnp.int32(0)
-        if turn == 0 or n_groups > 1:
-            delta = jnp.zeros((8, BLOCK), jnp.float32)
-        else:
-            early = (2 * place) // group
-            delta = lax.fori_loop(0, early, pass_block, jnp.zeros((8, BLOCK), jnp.float32))
         for away in range(1, n_unit):
             mate_copy(turn, away).wait_recv()
             held = mates[turn, away - 1]
@@ -239,6 +245,10 @@
             def _():
                 coef_copy(turn, away).start()
 
+        spread(group - 1, [own[index] for index in range(COEFS)])
+        ahead = jnp.where(time < group, 0, jnp.maximum(place - turn, 0))
+        lax.fori_loop(0, ahead, prepare_ahead, 0)
+        delta = jnp.zeros((8, BLOCK), jnp.float32)
         if n_groups > 1:
             relay_in_now = relay_in.at[turn]
 
@@ -251,11 +261,10 @@
                 relay_copy(turn, 0).wait_recv()
 
             delta = relay_in_now[...]
-        delta = lax.fori_loop(early, place, pass_block, delta)
+        delta = lax.fori_loop(0, place, pass_block, delta)
         moves[0:blocks, :] = delta[:blocks]
-        table = own[...]
         for t in range(steps):
-            delta = step(delta, at_step(table, t))
+            delta = step(delta, at_step(group - 1, t))
             moves[(t + 1) * blocks : (t + 2) * blocks, :] = delta[:blocks]
         if n_groups > 1:
             relay_out[turn] = delta
@@ -321,6 +330,7 @@
             pltpu.VMEM((COEFS, rows, BLOCK), f32),
             pltpu.VMEM((NEWTON, SENT, rows, BLOCK), bf16),
             pltpu.VMEM((NEWTON, group - 1, SENT, rows, BLOCK), bf16),
+            pltpu.VMEM((group, COEFS, steps, 8, BLOCK), f32),
             pltpu.VMEM((rows + 8, BLOCK), f32),
             pltpu.VMEM((NEWTON, 8, BLOCK), f32),
             pltpu.VMEM((NEWTON, 8, BLOCK), f32),

time: 22.5 us -> 22.5 us (level)
  no operation moved by 1% of the time
where the time goes in v8:
time: 22.5 us; the launch traced here: 22.1 us
  Pallas kernels  20.8 us (92%)
  local copies, waits for them, and re-layouts  1.3 us (6%)
    pallas_call x1, Pallas kernels, shards(): pl.pallas_call(functools.partial(newton_kernel, n_tm, n_unit), out_shape=...  20.8 us
    unnamed x1, local copies, waits for them, and re-layouts  1.3 us

profile of v8, /device:TPU:31, one launch (start us, length us, event | category | flops | bytes accessed | tf_op | source)
XLA Modules:
  0.0 22.1 jit_solution(4624380638783490685)
XLA Ops:
  0.0 20.8 %newton.1 = f32[4,512]{1,0:T(4,128)} custom-call(bf16[3,4,512]{2,1,0:T(4,128)(2,1)} %bitcast.10, bf16[3,1024,512]{2,1,0:T(8,128)(2,1)} %bitcast.8, f32[1,512]{1,0:T(1,128)} %bitcast.12, f32[1,512]{1,0:T(1,128)} %bitcast.13, f32[1,512]{1,0:T(1,128)} %start_hbm.1, f32[4,512]{1,0:T(4,128)} %bitcast.11), custom_call_target="tpu_custom_call" | custom-call | tf_op jit(solution)/shard_map/newton/pallas_call | solution.py:316
  20.8 1.3 %copy.8 = f32[1,4,512]{2,1,0:T(4,128)} copy(f32[1,4,512]{2,1,0:T(4,128)} %bitcast.9) | data formatting | bytes 16384

commit v9 on v7

--- a/solution.py
+++ b/solution.py
@@ -159,13 +159,12 @@
             left = jnp.concatenate(
                 [jnp.where((row % side == depth) & (row < blocks), delta, 0.0) for depth in range(side)], axis=1
             ).astype(jnp.bfloat16)
-            terms = jnp.dot(left, w_diag[...], preferred_element_type=jnp.float32)
 
             def of_gate(gate):
                 value = None
                 for pair in range(blocks // side):
                     column = gate_column(pair, gate)
-                    part = terms[:, column : column + BLOCK]
+                    part = jnp.dot(left, w_diag[:, column : column + BLOCK], preferred_element_type=jnp.float32)
                     value = part if value is None else jnp.where(row // side == pair, part, value)
                 return value
 

time: 22.5 us -> 22.4 us (level)
  no operation moved by 1% of the time
where the time goes in v9:
time: 22.4 us; the launch traced here: 22 us
  Pallas kernels  20.7 us (92%)
  local copies, waits for them, and re-layouts  1.3 us (6%)
    pallas_call x1, Pallas kernels, shards(): pl.pallas_call(functools.partial(newton_kernel, n_tm, n_unit), out_shape=...  20.7 us
    unnamed x1, local copies, waits for them, and re-layouts  1.3 us

profile of v9, /device:TPU:31, one launch (start us, length us, event | category | flops | bytes accessed | tf_op | source)
XLA Modules:
  0.0 22.0 jit_solution(9195973859862043672)
XLA Ops:
  0.0 20.7 %newton.1 = f32[4,512]{1,0:T(4,128)} custom-call(bf16[3,4,512]{2,1,0:T(4,128)(2,1)} %bitcast.10, bf16[3,1024,512]{2,1,0:T(8,128)(2,1)} %bitcast.8, f32[1,512]{1,0:T(1,128)} %bitcast.12, f32[1,512]{1,0:T(1,128)} %bitcast.13, f32[1,512]{1,0:T(1,128)} %start_hbm.1, f32[4,512]{1,0:T(4,128)} %bitcast.11), custom_call_target="tpu_custom_call" | custom-call | tf_op jit(solution)/shard_map/newton/pallas_call | solution.py:306
  20.7 1.3 %copy.8 = f32[1,4,512]{2,1,0:T(4,128)} copy(f32[1,4,512]{2,1,0:T(4,128)} %bitcast.9) | data formatting | bytes 16384

commit v10 on v7

--- a/solution.py
+++ b/solution.py
@@ -198,10 +198,10 @@
 
         rec = product(previous, unit)
         early = jnp.int32(0)
-        if turn == 0 or n_groups > 1:
+        if turn == 0:
             delta = jnp.zeros((8, BLOCK), jnp.float32)
         else:
-            early = (2 * place) // group
+            early = jnp.where(time < group, lax.div(2 * place, group), 0)
             delta = lax.fori_loop(0, early, pass_block, jnp.zeros((8, BLOCK), jnp.float32))
         for away in range(1, n_unit):
             mate_copy(turn, away).wait_recv()
@@ -244,7 +244,7 @@
 
             @pl.when(time < group)
             def _():
-                relay_in_now[...] = jnp.zeros((8, BLOCK), jnp.float32)
+                relay_in_now[...] = delta
 
             @pl.when(time >= group)
             def _():

time: 22.5 us -> 22.9 us (1.018)
  the two profiles are of different devices: /device:TPU:31 before, /device:TPU:24 now
where the time goes in v10:
time: 22.9 us; the launch traced here: 22.6 us
  Pallas kernels  21.3 us (93%)
  local copies, waits for them, and re-layouts  1.3 us (6%)
    pallas_call x1, Pallas kernels, shards(): pl.pallas_call(functools.partial(newton_kernel, n_tm, n_unit), out_shape=...  21.3 us
    unnamed x1, local copies, waits for them, and re-layouts  1.3 us

profile of v10, /device:TPU:24, one launch (start us, length us, event | category | flops | bytes accessed | tf_op | source)
XLA Modules:
  0.0 22.6 jit_solution(4101794687896031742)
XLA Ops:
  0.0 21.3 %newton.1 = f32[4,512]{1,0:T(4,128)} custom-call(bf16[3,4,512]{2,1,0:T(4,128)(2,1)} %bitcast.10, bf16[3,1024,512]{2,1,0:T(8,128)(2,1)} %bitcast.8, f32[1,512]{1,0:T(1,128)} %bitcast.12, f32[1,512]{1,0:T(1,128)} %bitcast.13, f32[1,512]{1,0:T(1,128)} %start_hbm.1, f32[4,512]{1,0:T(4,128)} %bitcast.11), custom_call_target="tpu_custom_call" | custom-call | tf_op jit(solution)/shard_map/newton/pallas_call | solution.py:307
  21.3 1.3 %copy.8 = f32[1,4,512]{2,1,0:T(4,128)} copy(f32[1,4,512]{2,1,0:T(4,128)} %bitcast.9) | data formatting | bytes 16384
